TPU v7x, 512 devices: a whole 4x4x16 slice. The times are simulated.
512 devices in a mesh: dp: 16 (over z), expert: 32 (over y, x, core).
Axes of the slice: x: 4, y: 4, z: 16, core: 2. Of those that a mesh axis runs over, the one named last changes fastest.
Arguments:
- activations: bfloat16 [65536, 3584], P(('dp', 'expert')), may hold values from -6 to 6
- out_grad: bfloat16 [65536, 3584], P(('dp', 'expert')), may hold values from -0.09375 to 0.09375
- router_weight: bfloat16 [128, 3584], P('expert'), may hold values from -0.09375 to 0.09375
- expert_ids: int32 [65536, 2], P(('dp', 'expert')), may hold values from 0 to 127, all different within a row; in each aligned block of 128 rows (0 to 127, 128 to 255, ...) at most 2 rows name the same one
- saved_output: bfloat16 [16, 128, 64, 3584], P('dp', 'expert'), may hold values from -6 to 6
Outputs:
- input_grad: bfloat16 [65536, 3584], P(('dp', 'expert'))
- score_grad: float32 [65536, 2], P(('dp', 'expert'))
- router_grad: float32 [128, 3584], P('expert')
Inputs may be any that keep to these rules, and one draw needn't show every extreme that they name: `expert_ids`: within the 128 rows of one device no expert is named more than 2 times; a row names distinct experts.
All inputs are finite; a program needn't handle non-finite values.
Results may differ from a plain program's by a relative error of at most 0.0049.
Values may be sent and summed in bfloat16 or wider, within the bound.
No kernel may reach another device: no remote copies, remote signals or barrier semaphores. Data moves between devices by JAX's collectives and lax.ppermute only.
A program may use at most 64 MiB of HBM per device.

v0:
```python
import jax
import jax.numpy as jnp
from jax import lax
from jax.sharding import PartitionSpec as P

route_scale = 2.5


def body(activations, out_grad, router_weight, expert_ids, saved_output):
    owners = lax.axis_size("expert")
    local_experts = router_weight.shape[0]
    experts_all = local_experts * owners
    width = activations.shape[1]
    capacity = saved_output.shape[2] // owners
    expert_axis = jnp.arange(experts_all, dtype=jnp.int32)
    onehot = (expert_ids[:, :, None] == expert_axis[None, None, :]).astype(jnp.int32)
    per_token = jnp.sum(onehot, axis=1)
    earlier = jnp.cumsum(per_token, axis=0) - per_token
    slot_index = jnp.sum(onehot * earlier[:, None, :], axis=2)
    position = expert_ids * capacity + slot_index
    slot_axis = jnp.arange(experts_all * capacity, dtype=jnp.int32)
    placing = (position[:, :, None] == slot_axis[None, None, :]).astype(jnp.float32)
    placer = jnp.sum(placing, axis=1).T.astype(jnp.bfloat16)
    router_full = lax.all_gather(router_weight, "expert", axis=0, tiled=True)
    logits = lax.dot_general(
        activations, router_full, (((1,), (1,)), ((), ())), preferred_element_type=jnp.float32
    )
    onehot_f = onehot.astype(jnp.float32)
    chosen = jnp.sum(onehot_f * logits[:, None, :], axis=2)
    score = jax.nn.sigmoid(chosen)
    total = jnp.sum(score, axis=1, keepdims=True)
    saved = saved_output.reshape(local_experts, owners, capacity, width)
    outgoing = jnp.dot(placer, out_grad, preferred_element_type=jnp.float32).astype(jnp.bfloat16)
    outgoing = outgoing.reshape(experts_all, 1, capacity, width)
    arrived = lax.all_to_all(outgoing, "expert", split_axis=0, concat_axis=1, tiled=True)
    inner = jnp.einsum("esmd,esmd->esm", arrived, saved, preferred_element_type=jnp.float32)
    returned = lax.all_to_all(inner, "expert", split_axis=1, concat_axis=0, tiled=True).reshape(
        experts_all * capacity
    )
    gate_dots = jnp.sum(placing * returned[None, None, :], axis=2)
    mean_term = jnp.sum(score * gate_dots, axis=1, keepdims=True) / total
    score_grad = route_scale / total * (gate_dots - mean_term) * score * (1.0 - score)
    grad_low = score_grad.astype(jnp.bfloat16)
    dense = jnp.sum(onehot_f * grad_low.astype(jnp.float32)[:, :, None], axis=1).astype(
        jnp.bfloat16
    )
    input_grad = jnp.dot(dense, router_full, preferred_element_type=jnp.float32).astype(
        jnp.bfloat16
    )
    local_rows = lax.psum_scatter(
        lax.dot_general(
            dense, activations, (((0,), (0,)), ((), ())), preferred_element_type=jnp.float32
        ),
        "expert",
        scatter_dimension=0,
        tiled=True,
    )
    router_grad = lax.psum(local_rows, "dp")
    return (input_grad, score_grad, router_grad)


def solution(mesh):
    in_specs = (
        P(("dp", "expert"), None),
        P(("dp", "expert"), None),
        P("expert", None),
        P(("dp", "expert"), None),
        P("dp", "expert", None, None),
    )
    out_specs = (P(("dp", "expert"), None), P(("dp", "expert"), None), P("expert", None))
    return jax.shard_map(body, mesh=mesh, in_specs=in_specs, out_specs=out_specs, check_vma=False)
```

profile of v0, /device:TPU:6, one launch (start us, length us, event | category | flops | bytes accessed | tf_op | source)
XLA Modules:
  0.0 288.2 jit_solution(1980374221727902111)
XLA Ops:
  7.2 0.0 copy-start
  7.2 0.9 convert_reduce_fusion.1
  8.0 0.2 reduce_window_sum.11
  8.2 0.9 select_reduce_fusion.1
  9.1 0.7 multiply_add_fusion
  9.8 0.1 convert_reduce_fusion
  9.9 0.0 copy-done
  9.9 0.7 convolution_convert_fusion
  10.6 1.7 reshape.79
  12.2 0.0 copy-start.2
  12.2 10.3 %all-to-all-start = ((bf16[128,1,2,3584]{3,2,1,0:T(2,128)(2,1)}), bf16[128,1,2,3584]{3,2,1,0:T(2,128)(2,1)}, u32[]{:S(2)}, u32[]{:S(2)}) async-start(bf16[128,1,2,3584]{3,2,1,0:T(2,128)(2,1)} %bitcast.1), calls=%async_computation | async-start | bytes 3670016 | tf_op jit(solution)/shard_map/all_to_all | solution.py:35
  22.6 0.0 copy-done.2
  22.6 0.0 copy-start.3
  22.6 1.7 reshape.80
  24.2 0.0 copy-done.3
  24.2 39.7 %all-gather = bf16[32,4,3584]{2,1,0:T(4,128)(2,1)S(1)} all-gather(bf16[1,4,3584]{2,1,0:T(4,128)(2,1)S(1)} %bitcast.24), channel_id=1, replica_groups=mesh['dp'=16,'expert'=32] {'expert'}, dimensions={0}, use_global_device_ids=true | all-gather | bytes 946176 | tf_op jit(solution)/shard_map/all_gather | solution.py:24
  63.9 0.2 reshape.82
  64.2 1.6 fusion.9
  65.7 0.0 all-to-all-done
  65.7 0.0 copy-start.4
  65.8 0.0 copy-start.1
  65.8 4.6 %multiply_reduce_fusion = f32[4,32,2]{2,1,0:T(8,128)S(1)} fusion(bf16[4,32,2,3584]{3,2,1,0:T(2,128)(2,1)} %reshape.80, bf16[4,32,2,3584]{3,2,0,1:T(2,128)(2,1)} %bitcast.4), kind=kLoop, calls=%fused_computation.2 | loop fusion | flops 3669760 | bytes 3671040
  70.3 0.9 copy.25
  71.3 5.6 %all-to-all-start.1 = ((f32[4,32,2]{0,2,1:T(2,128)}), f32[4,32,2]{0,2,1:T(2,128)S(1)}, u32[]{:S(2)}, u32[]{:S(2)}) async-start(f32[4,32,2]{0,2,1:T(2,128)} %copy.25), calls=%async_computation.1 | async-start | bytes 65536 | tf_op jit(solution)/shard_map/all_to_all | solution.py:37
  76.9 0.0 all-reduce.3.cloned.1.call-start
  76.9 0.0 copy-done.4
  76.9 0.2 fusion.2
  77.1 5.4 %all-to-all-done.1 = f32[4,32,2]{0,2,1:T(2,128)S(1)} async-done(((f32[4,32,2]{0,2,1:T(2,128)}), f32[4,32,2]{0,2,1:T(2,128)S(1)}, u32[]{:S(2)}, u32[]{:S(2)}) %all-to-all-start.1) | async-done | bytes 1056 | tf_op jit(solution)/shard_map/all_to_all | solution.py:37
  82.5 0.3 copy.20
  82.8 0.1 mul.76
  82.9 0.2 select_reduce_fusion
  83.2 0.6 convert_convert_fusion.1
  83.7 0.1 fusion.3
  83.9 0.0 copy-done.1
  83.9 1.7 fusion.10
  85.5 0.0 all-reduce.3.cloned.1.call-update
  85.6 1.3 dynamic-slice
  87.5 1.3 convolution_convert_fusion.1
  88.8 134.1 %all-reduce.3.cloned.1.call-done = f32[128,3584]{1,0:T(8,128)} async-done(((f32[128,3584]{1,0:T(8,128)}), f32[128,3584]{1,0:T(8,128)}) %all-reduce.3.cloned.1.call-update) | async-done | bytes 1835024
  222.9 0.9 constant_dynamic-slice_fusion
  223.8 57.5 %psum.7 = f32[4,3584]{1,0:T(4,128)} all-reduce(f32[4,3584]{1,0:T(4,128)S(1)} %constant_dynamic-slice_fusion), channel_id=1, replica_groups=mesh['dp'=16,'expert'=32] {'dp'}, use_global_device_ids=true, to_apply=%region_10.11 | all-reduce | flops 14336 | bytes 114688 | tf_op jit(solution)/shard_map/psum | solution.py:58
  (3 shorter events, 0.0 us)
Async XLA Ops:
  7.2 2.7 copy-start
  12.2 10.3 %copy-start.2 = (bf16[1,4,64,3584]{3,2,1,0:T(8,128)(2,1)S(1)}, bf16[1,4,64,3584]{3,2,1,0:T(8,128)(2,1)}, u32[]{:S(2)}) copy-start(bf16[1,4,64,3584]{3,2,1,0:T(8,128)(2,1)} %param.9) | copy-start | bytes 5505028
  12.2 53.5 %all-to-all-start = ((bf16[128,1,2,3584]{3,2,1,0:T(2,128)(2,1)}), bf16[128,1,2,3584]{3,2,1,0:T(2,128)(2,1)}, u32[]{:S(2)}, u32[]{:S(2)}) async-start(bf16[128,1,2,3584]{3,2,1,0:T(2,128)(2,1)} %bitcast.1), calls=%async_computation | async-start | bytes 3670016 | tf_op jit(solution)/shard_map/all_to_all | solution.py:35
  22.6 1.7 copy-start.3
  65.7 11.2 %copy-start.4 = (s32[128,2]{0,1:T(2,128)S(1)}, s32[128,2]{0,1:T(2,128)}, u32[]{:S(2)}) copy-start(s32[128,2]{0,1:T(2,128)} %param.8) | copy-start | bytes 3076
  65.8 18.1 %copy-start.1 = (bf16[128,3584]{1,0:T(8,128)(2,1)S(1)}, bf16[128,3584]{1,0:T(8,128)(2,1)}, u32[]{:S(2)}) copy-start(bf16[128,3584]{1,0:T(8,128)(2,1)} %param.5) | copy-start | bytes 2752516
  71.3 11.2 %all-to-all-start.1 = ((f32[4,32,2]{0,2,1:T(2,128)}), f32[4,32,2]{0,2,1:T(2,128)S(1)}, u32[]{:S(2)}, u32[]{:S(2)}) async-start(f32[4,32,2]{0,2,1:T(2,128)} %copy.25), calls=%async_computation.1 | async-start | bytes 65536 | tf_op jit(solution)/shard_map/all_to_all | solution.py:37
  76.9 146.0 %all-reduce.3.cloned.1.call-start = ((), (), s32[]{:S(2)}) async-start(), calls=%async_computation.2 | async-start | bytes 3670016
Sparse Core Ops, SparseCore 0:
  85.7 137.1 all-reduce.2
where the time goes:
time: 289 us; the launch traced here: 288 us
  waiting for transfers between devices  139 us (48%)
  blocking collectives  97.2 us (34%)
  starting transfers between devices  16 us (6%)
  between operations  14.8 us (5%)
  other arithmetic  8.37 us (3%)
  local copies, waits for them, and re-layouts  7.1 us (2%)
  matrix products  5.19 us (2%)
    unnamed x2, waiting for transfers between devices  134 us
    psum x1, blocking collectives, body(): router_grad = lax.psum(local_rows, 'dp')  57.5 us
    all_gather x1, blocking collectives, body(): router_full = lax.all_gather(router_weight, 'expert', axis=0, tiled=True)  39.7 us
    all_to_all x1, starting transfers between devices, body(): lax.all_to_all(outgoing, 'expert', split_axis=0, concat_axis=1, tiled=True)  10.3 us
  transfers between devices with their start and end apart: 3, of which 2 were waited for; matrix products, arithmetic and copies ran while one was open for 2% of the time, Pallas kernels for 0%

commit v1 on v0

v1 whole, which is shorter than its diff:
```python
import jax
import jax.numpy as jnp
from jax import lax
from jax.experimental import pallas as pl
from jax.experimental.pallas import tpu as pltpu
from jax.sharding import Mesh, PartitionSpec as P

route_scale = 2.5
BF16, F32 = jnp.bfloat16, jnp.float32
NT = (((1,), (1,)), ((), ()))
TN = (((0,), (0,)), ((), ()))


def iota(shape, dim):
    return lax.broadcasted_iota(jnp.int32, shape, dim)


def pack_kernel(saved_steps, saved_ref, weight_ref, out_ref):
    rows, block = out_ref.shape
    experts, width = weight_ref.shape
    capacity = rows // (rows // (2 * experts)) // experts
    owners = rows // (experts * capacity)
    step = pl.program_id(0)
    row = iota((rows, rows), 0)
    col = iota((rows, rows), 1)

    @pl.when(step < saved_steps)
    def _():
        dest = row // (experts * capacity)
        local = row % (experts * capacity)
        source = (local // capacity) * (owners * capacity) + dest * capacity + local % capacity
        pick = (col == source).astype(F32).astype(BF16)
        out_ref[...] = jnp.dot(pick, saved_ref[...], preferred_element_type=F32).astype(BF16)

    for part in range(width // 2 // block):

        @pl.when(step == saved_steps + part)
        def _(part=part):
            r = iota((rows, experts), 0)
            e = iota((rows, experts), 1)
            total = jnp.zeros((rows, block), F32)
            for half in range(2):
                pick = (r % (2 * experts) == 2 * e + half).astype(F32).astype(BF16)
                piece = weight_ref[:, pl.ds(half * (width // 2) + part * block, block)]
                total += jnp.dot(pick, piece, preferred_element_type=F32)
            out_ref[...] = total.astype(BF16)


def pack(saved, weight):
    rows, width = saved.shape
    block = width // 4
    steps = 4 + 2
    return pl.pallas_call(
        lambda *refs: pack_kernel(4, *refs),
        grid=(steps,),
        in_specs=[
            pl.BlockSpec((rows, block), lambda j: (0, jnp.minimum(j, 3))),
            pl.BlockSpec(weight.shape, lambda j: (0, 0)),
        ],
        out_specs=pl.BlockSpec((rows, block), lambda j: (0, j)),
        out_shape=jax.ShapeDtypeStruct((rows, steps * block), BF16),
        name="pack_rows",
    )(saved, weight)


def score_kernel(ids_ref, got_ref, act_ref, grad_ref, score_grad_ref, spread_ref, part_ref):
    rows = got_ref.shape[0]
    tokens, width = act_ref.shape
    half = width // 2
    quarter = width // 4
    ids = ids_ref[...]
    col = iota((rows, tokens), 0)
    odd = (col % 2).astype(F32)
    named = [(col // 2 == ids[k : k + 1, :]) for k in range(2)]
    both = jnp.where(named[0] | named[1], 1.0, 0.0).astype(BF16)
    before = (iota((tokens, tokens), 0) < iota((tokens, tokens), 1)).astype(F32).astype(BF16)
    earlier = jnp.dot(both, before, preferred_element_type=F32)
    dots = lax.dot_general(got_ref[:, :width], grad_ref[...], NT, preferred_element_type=F32)
    dots = jnp.where(earlier == odd, dots, 0.0)
    low = lax.dot_general(
        got_ref[:, width:], act_ref[:, :half], NT, preferred_element_type=F32
    )
    high = lax.dot_general(
        got_ref[:, width:], act_ref[:, half:], NT, preferred_element_type=F32
    )
    logits = jnp.where(odd == 1.0, high, low)
    score, gate = [], []
    for k in range(2):
        chosen = jnp.sum(jnp.where(named[k], logits, 0.0), axis=0, keepdims=True)
        score.append(jax.nn.sigmoid(chosen))
        gate.append(jnp.sum(jnp.where(named[k], dots, 0.0), axis=0, keepdims=True))
    total = score[0] + score[1]
    mean_term = (score[0] * gate[0] + score[1] * gate[1]) / total
    dense = jnp.zeros((rows, tokens), F32)
    for k in range(2):
        grad = route_scale / total * (gate[k] - mean_term) * score[k] * (1.0 - score[k])
        score_grad_ref[k : k + 1, :] = grad
        dense = jnp.where(named[k], grad, dense)
    even_part = jnp.where(odd == 0.0, dense, 0.0).astype(BF16)
    odd_part = jnp.where(odd == 1.0, dense, 0.0).astype(BF16)
    spread_ref[:rows, :] = even_part
    spread_ref[rows:, :] = odd_part
    for side in range(2):
        out = jnp.dot(
            even_part,
            act_ref[:, side * half : side * half + quarter],
            preferred_element_type=F32,
        ) + jnp.dot(
            odd_part,
            act_ref[:, side * half + quarter : (side + 1) * half],
            preferred_element_type=F32,
        )
        part_ref[side * rows : (side + 1) * rows, :] = out.astype(BF16)


def scores(ids, got, act, grad):
    rows = got.shape[0]
    tokens, width = act.shape
    return pl.pallas_call(
        score_kernel,
        out_shape=(
            jax.ShapeDtypeStruct((2, tokens), F32),
            jax.ShapeDtypeStruct((2 * rows, tokens), BF16),
            jax.ShapeDtypeStruct((2 * rows, width // 4), BF16),
        ),
        compiler_params=pltpu.CompilerParams(vmem_limit_bytes=40 * 1024 * 1024),
        name="scores",
    )(ids, got, act, grad)


def input_kernel(spread_ref, weight_ref, out_ref):
    out_ref[...] = lax.dot_general(
        spread_ref[...], weight_ref[...], TN, preferred_element_type=F32
    ).astype(BF16)


def input_grads(spread, got, width):
    rows = got.shape[0]
    tokens = spread.shape[1]
    block = width // 4
    return pl.pallas_call(
        input_kernel,
        grid=(4,),
        in_specs=[
            pl.BlockSpec((rows, tokens), lambda j: (j // 2, 0)),
            pl.BlockSpec((rows, block), lambda j: (0, 4 + j % 2)),
        ],
        out_specs=pl.BlockSpec((tokens, block), lambda j: (0, j)),
        out_shape=jax.ShapeDtypeStruct((tokens, width), BF16),
        cost_estimate=pl.CostEstimate(
            flops=2 * tokens * rows * width, bytes_accessed=4 * tokens * width, transcendentals=0
        ),
        name="input_grads",
    )(spread, got)


def sum_kernel(got_ref, out_ref):
    rows, sources = out_ref.shape[0], got_ref.shape[0]
    pick = (iota((rows, sources), 0) % 8 == iota((rows, sources), 1) % 8).astype(F32).astype(BF16)
    out_ref[...] = jnp.dot(pick, got_ref[...], preferred_element_type=F32).astype(BF16)


def final_kernel(got_ref, out_ref):
    experts, width = out_ref.shape
    sources, block = got_ref.shape
    row = iota((experts, sources), 0)
    col = iota((experts, sources), 1) % (4 * experts)
    for piece in range(width // block):
        want = (piece // 2) * 2 * experts + row * 2 + piece % 2
        pick = (col == want).astype(F32).astype(BF16)
        out_ref[:, piece * block : (piece + 1) * block] = jnp.dot(
            pick, got_ref[...], preferred_element_type=F32
        )


def body(activations, out_grad, router_weight, expert_ids, saved_output):
    experts, width = router_weight.shape
    planes = lax.axis_size("pairs") * lax.axis_size("side")
    saved = saved_output.reshape(experts * saved_output.shape[2], width)
    packed = pack(saved, router_weight)
    got = lax.all_to_all(packed, "expert", split_axis=0, concat_axis=0, tiled=True)
    score_grad, spread, part = scores(expert_ids.T, got, activations, out_grad)
    part = lax.all_to_all(part, ("side", "expert"), split_axis=0, concat_axis=0, tiled=True)
    input_grad = input_grads(spread, got, width)
    rows = 2 * experts
    summed = pl.pallas_call(
        sum_kernel,
        out_shape=jax.ShapeDtypeStruct((planes * rows, width // 4), BF16),
        name="sum_planes",
    )(part)
    summed = lax.all_to_all(summed, ("pairs", "side"), split_axis=0, concat_axis=0, tiled=True)
    router_grad = pl.pallas_call(
        final_kernel,
        out_shape=jax.ShapeDtypeStruct((experts, width), F32),
        name="sum_batches",
    )(summed)
    return input_grad, score_grad.T, router_grad


def solution(mesh):
    dp, owners = mesh.shape["dp"], mesh.shape["expert"]
    mesh = Mesh(mesh.devices.reshape(dp // 2, 2, owners), ("pairs", "side", "expert"))
    tokens = P(("pairs", "side", "expert"), None)
    in_specs = (
        tokens,
        tokens,
        P("expert", None),
        tokens,
        P(("pairs", "side"), "expert", None, None),
    )
    out_specs = (tokens, tokens, P("expert", None))
    return jax.shard_map(body, mesh=mesh, in_specs=in_specs, out_specs=out_specs, check_vma=False)
```

time: 289 us -> 109 us (0.38)
  waiting for transfers between devices: 139 us -> 13.2 us
  blocking collectives: 97.2 us -> 64.7 us
  Pallas kernels: 0 us -> 15.3 us
  between operations: 14.8 us -> 0.67 us
  other arithmetic: 8.37 us -> 0 us
  local copies, waits for them, and re-layouts: 7.1 us -> 0.7 us
  matrix products: 5.19 us -> 0 us
  starting transfers between devices: 16 us -> 13.1 us
    unnamed x2 -> x0, waiting for transfers between devices: 134 us -> none
    all_to_all x0 -> x2, blocking collectives: none -> 64.7 us  [the longest x1 43 us: body(): lax.all_to_all(packed, 'expert', split_axis=0, concat_axis=0, tiled=True)]
    psum x1 -> x0, blocking collectives: 57.5 us -> none  [body(): router_grad = lax.psum(local_rows, 'dp')]
    all_gather x1 -> x0, blocking collectives: 39.7 us -> none  [body(): router_full = lax.all_gather(router_weight, 'expert', axis=0, tiled=True)]
    pallas_call x0 -> x5, Pallas kernels: none -> 15.3 us  [the longest x1 5.51 us: pack(): pl.pallas_call(lambda *refs: pack_kernel(4, *refs), grid=(steps,), in_spe...]
    all_to_all x2 -> x1, waiting for transfers between devices: 5.36 us -> 13.2 us  [body(): lax.all_to_all(summed, ('pairs', 'side'), split_axis=0, concat_axis=0, ti...]
    dot_general x4 -> x0, matrix products: 5.19 us -> none  [the longest x1 1.65 us: body(): lax.dot_general(dense, activations, (((0,), (0,)), ((), ())), preferred_e...]
    unnamed x1 -> x0, other arithmetic: 4.57 us -> none
  transfers between devices with their start and end apart: 3 -> 1, of which waited for: 2 -> 1; matrix products, arithmetic and copies ran while one was open for 2% -> 0% of each run, Pallas kernels for 0% -> 4%
where the time goes in v1:
time: 109 us; the launch traced here: 108 us
  blocking collectives  64.7 us (59%)
  Pallas kernels  15.3 us (14%)
  waiting for transfers between devices  13.2 us (12%)
  starting transfers between devices  13.1 us (12%)
    all_to_all x1, blocking collectives, body(): lax.all_to_all(packed, 'expert', split_axis=0, concat_axis=0, tiled=True)  43 us
    all_to_all x1, blocking collectives, body(): lax.all_to_all(part, ('side', 'expert'), split_axis=0, concat_axis=0, til...  21.8 us
    all_to_all x1, waiting for transfers between devices, body(): lax.all_to_all(summed, ('pairs', 'side'), split_axis=0, concat_axis=0, ti...  13.2 us
    all_to_all x1, starting transfers between devices, body(): lax.all_to_all(summed, ('pairs', 'side'), split_axis=0, concat_axis=0, ti...  13.1 us
    pallas_call x1, Pallas kernels, pack(): pl.pallas_call(lambda *refs: pack_kernel(4, *refs), grid=(steps,), in_spe...  5.51 us
    pallas_call x1, Pallas kernels, input_grads(): pl.pallas_call(input_kernel, grid=(4,), in_specs=[pl.BlockSpec((rows, tok...  4.03 us
  transfers between devices with their start and end apart: 1, of which 1 were waited for; matrix products, arithmetic and copies ran while one was open for 0% of the time, Pallas kernels for 4%

profile of v1, /device:TPU:6, one launch (start us, length us, event | category | flops | bytes accessed | tf_op | source)
XLA Modules:
  0.0 107.7 jit_solution(12094903831227803907)
XLA Ops:
  0.6 5.5 %pack_rows.1 = bf16[256,5376]{1,0:T(8,128)(2,1)} custom-call(bf16[256,3584]{1,0:T(8,128)(2,1)} %bitcast.15, bf16[4,3584]{1,0:T(4,128)(2,1)} %refs_1_.1), custom_call_target="tpu_custom_call" | custom-call | tf_op jit(solution)/shard_map/pack_rows/pallas_call | solution.py:53
  6.1 0.0 copy-start.1
  6.1 0.0 copy-start.2
  6.1 0.0 copy-start.4
  6.1 43.0 %all_to_all.33 = bf16[32,8,5376]{2,1,0:T(8,128)(2,1)S(1)} all-to-all(bf16[32,8,5376]{2,1,0:T(8,128)(2,1)} %bitcast.13), channel_id=1, replica_groups=mesh['pairs'=8,'side'=2,'expert'=32] {'expert'}, dimensions={0} | all-to-all | bytes 5505024 | tf_op jit(solution)/shard_map/all_to_all | solution.py:181
  49.1 0.0 copy-start
  49.1 0.0 copy-done.1
  49.1 0.0 copy-done.2
  49.1 0.0 copy-done.4
  49.1 1.8 %scores.1 = (f32[2,128]{1,0:T(2,128)}, bf16[512,128]{1,0:T(8,128)(2,1)S(1)}, bf16[512,896]{1,0:T(8,128)(2,1)S(1)}) custom-call(s32[2,128]{1,0:T(2,128)S(1)} %bitcast.12, bf16[256,5376]{1,0:T(8,128)(2,1)S(1)} %bitcast.9, bf16[128,3584]{1,0:T(8,128)(2,1)S(1)} %copy-done.1, bf16[128,3584]{1,0:T(8,128)(2,1)S(1)} %copy-done.2), custom_call_target="tpu_custom_call" | custom-call | tf_op jit(solution)/shard_map/scores/pallas_call | solution.py:119
  50.9 0.0 copy-start.3
  50.9 21.8 %all_to_all.34 = bf16[64,8,896]{2,1,0:T(8,128)(2,1)} all-to-all(bf16[64,8,896]{2,1,0:T(8,128)(2,1)S(1)} %bitcast.11), channel_id=1, replica_groups=mesh['pairs'=8,'side'=2,'expert'=32] {'side','expert'}, dimensions={0} | all-to-all | bytes 1835008 | tf_op jit(solution)/shard_map/all_to_all | solution.py:183
  72.7 0.0 copy-done
  72.7 0.0 copy-done.3
  72.7 2.2 %sum_planes.1 = bf16[128,896]{1,0:T(8,128)(2,1)} custom-call(bf16[512,896]{1,0:T(8,128)(2,1)} %bitcast.14), custom_call_target="tpu_custom_call" | custom-call | tf_op jit(solution)/shard_map/sum_planes/pallas_call | solution.py:186
  74.9 13.1 %all-to-all-start.2 = ((bf16[16,8,896]{2,1,0:T(8,128)(2,1)}), bf16[16,8,896]{2,1,0:T(8,128)(2,1)S(1)}, u32[]{:S(2)}, u32[]{:S(2)}) async-start(bf16[16,8,896]{2,1,0:T(8,128)(2,1)} %bitcast.17), calls=%async_computation.2 | async-start | bytes 458752 | tf_op jit(solution)/shard_map/all_to_all | solution.py:191
  88.0 4.0 %input_grads.1 = bf16[128,3584]{1,0:T(8,128)(2,1)} custom-call(bf16[512,128]{1,0:T(8,128)(2,1)} %copy-done.3, bf16[256,5376]{1,0:T(8,128)(2,1)} %bitcast.10), custom_call_target="tpu_custom_call" | custom-call | flops 234881024 | bytes 1835008 | tf_op jit(solution)/shard_map/input_grads/pallas_call | solution.py:141
  92.0 13.2 %all-to-all-done.2 = bf16[16,8,896]{2,1,0:T(8,128)(2,1)S(1)} async-done(((bf16[16,8,896]{2,1,0:T(8,128)(2,1)}), bf16[16,8,896]{2,1,0:T(8,128)(2,1)S(1)}, u32[]{:S(2)}, u32[]{:S(2)}) %all-to-all-start.2) | async-done | bytes 229408 | tf_op jit(solution)/shard_map/all_to_all | solution.py:191
  105.2 0.0 copy-start.5
  105.2 0.7 copy-done.5
  105.9 1.8 %sum_batches.1 = f32[4,3584]{1,0:T(4,128)} custom-call(bf16[128,896]{1,0:T(8,128)(2,1)} %bitcast.16), custom_call_target="tpu_custom_call" | custom-call | tf_op jit(solution)/shard_map/sum_batches/pallas_call | solution.py:192
Async XLA Ops:
  6.1 43.0 %copy-start.1 = (bf16[128,3584]{1,0:T(8,128)(2,1)S(1)}, bf16[128,3584]{1,0:T(8,128)(2,1)}, u32[]{:S(2)}) copy-start(bf16[128,3584]{1,0:T(8,128)(2,1)} %act_ref.1) | copy-start | bytes 2752516
  6.1 43.0 %copy-start.2 = (bf16[128,3584]{1,0:T(8,128)(2,1)S(1)}, bf16[128,3584]{1,0:T(8,128)(2,1)}, u32[]{:S(2)}) copy-start(bf16[128,3584]{1,0:T(8,128)(2,1)} %grad_ref.1) | copy-start | bytes 2752516
  6.1 43.0 %copy-start.4 = (s32[128,2]{0,1:T(2,128)S(1)}, s32[128,2]{0,1:T(2,128)}, u32[]{:S(2)}) copy-start(s32[128,2]{0,1:T(2,128)} %param.8) | copy-start | bytes 3076
  49.1 23.6 %copy-start = (bf16[32,8,5376]{2,1,0:T(8,128)(2,1)}, bf16[32,8,5376]{2,1,0:T(8,128)(2,1)S(1)}, u32[]{:S(2)}) copy-start(bf16[32,8,5376]{2,1,0:T(8,128)(2,1)S(1)} %all_to_all.33) | copy-start | bytes 8257540
  50.9 21.8 %copy-start.3 = (bf16[512,128]{1,0:T(8,128)(2,1)}, bf16[512,128]{1,0:T(8,128)(2,1)S(1)}, u32[]{:S(2)}) copy-start(bf16[512,128]{1,0:T(8,128)(2,1)S(1)} %get-tuple-element.6.spread_ref) | copy-start | bytes 393220
  74.9 30.3 %all-to-all-start.2 = ((bf16[16,8,896]{2,1,0:T(8,128)(2,1)}), bf16[16,8,896]{2,1,0:T(8,128)(2,1)S(1)}, u32[]{:S(2)}, u32[]{:S(2)}) async-start(bf16[16,8,896]{2,1,0:T(8,128)(2,1)} %bitcast.17), calls=%async_computation.2 | async-start | bytes 458752 | tf_op jit(solution)/shard_map/all_to_all | solution.py:191
  105.2 0.7 copy-start.5

commit v2 on v0

v2 whole, which is shorter than its diff:
```python
import jax
import jax.numpy as jnp
from jax import lax
from jax.experimental import pallas as pl
from jax.experimental.pallas import tpu as pltpu
from jax.sharding import Mesh, PartitionSpec as P

route_scale = 2.5
BF16, F32 = jnp.bfloat16, jnp.float32
NT = (((1,), (1,)), ((), ()))
TN = (((0,), (0,)), ((), ()))
BIG = pltpu.CompilerParams(vmem_limit_bytes=40 * 1024 * 1024)


def iota(shape, dim):
    return lax.broadcasted_iota(jnp.int32, shape, dim)


def ones_where(mask):
    return jnp.where(mask, 1.0, 0.0).astype(BF16)


def pack_kernel(saved_hbm, weight_hbm, out_ref, saved_ref, weight_ref, saved_sem, weight_sem):
    rows, width = saved_ref.shape
    half = width // 2
    blocks = [slice(h * half, (h + 1) * half) for h in range(2)]
    copies = [
        pltpu.make_async_copy(saved_hbm.at[:, block], saved_ref.at[:, block], saved_sem.at[h])
        for h, block in enumerate(blocks)
    ]
    copies.append(pltpu.make_async_copy(weight_hbm, weight_ref, weight_sem))
    for copy in copies:
        copy.start()
    row, col = iota((rows, rows), 0), iota((rows, rows), 1)
    pick = ones_where(col == ((row >> 1) & 3) * (rows // 4) + (row >> 3) * 2 + (row & 1))
    row, col = iota((rows, 8), 0), iota((rows, 8), 1)
    pick_weight = ones_where(col == ((row >> 1) & 3) + (row & 1) * 4)
    copies[2].wait()
    halves = jnp.concatenate([weight_ref[:, block] for block in blocks], axis=0)
    out_ref[:, width:] = jnp.dot(pick_weight, halves, preferred_element_type=F32).astype(BF16)
    for h, block in enumerate(blocks):
        copies[h].wait()
        out_ref[:, block] = jnp.dot(
            pick, saved_ref[:, block], preferred_element_type=F32
        ).astype(BF16)


def pack(saved, weight):
    rows, width = saved.shape
    return pl.pallas_call(
        pack_kernel,
        in_specs=[pl.BlockSpec(memory_space=pltpu.HBM)] * 2,
        out_shape=jax.ShapeDtypeStruct((rows, width + width // 2), BF16),
        scratch_shapes=[
            pltpu.VMEM((rows, width), BF16),
            pltpu.VMEM(weight.shape, BF16),
            pltpu.SemaphoreType.DMA((2,)),
            pltpu.SemaphoreType.DMA,
        ],
        compiler_params=BIG,
        name="pack_rows",
    )(*[pltpu.with_memory_space_constraint(a, pltpu.HBM) for a in (saved, weight)])


def named_rows(ids, rows):
    row = iota((rows, ids.shape[1]), 0)
    return [(row >> 1) == ids[k : k + 1, :] for k in range(2)]


def score_kernel(ids_ref, got_ref, act_ref, grad_ref, score_grad_ref, part_ref):
    rows = got_ref.shape[0]
    tokens, width = act_ref.shape
    half, quarter = width // 2, width // 4
    ids = ids_ref[...]
    named = named_rows(ids, rows)
    odd = (iota((rows, tokens), 0) & 1) == 1
    before = ones_where(iota((tokens, tokens), 0) < iota((tokens, tokens), 1))
    earlier = jnp.dot(ones_where(named[0] | named[1]), before, preferred_element_type=F32)
    dots = lax.dot_general(got_ref[:, :width], grad_ref[...], NT, preferred_element_type=F32)
    dots = jnp.where(earlier == jnp.where(odd, 1.0, 0.0), dots, 0.0)
    halves = jnp.concatenate([act_ref[:, :half], act_ref[:, half:]], axis=0)
    logits = lax.dot_general(got_ref[:, width:], halves, NT, preferred_element_type=F32)
    logits = jnp.where(odd, logits[:, tokens:], logits[:, :tokens])
    score, gate = [], []
    for k in range(2):
        chosen = jnp.sum(jnp.where(named[k], logits, 0.0), axis=0, keepdims=True)
        score.append(jax.nn.sigmoid(chosen))
        gate.append(jnp.sum(jnp.where(named[k], dots, 0.0), axis=0, keepdims=True))
    total = score[0] + score[1]
    mean_term = (score[0] * gate[0] + score[1] * gate[1]) / total
    dense = jnp.zeros((rows, tokens), F32)
    for k in range(2):
        grad = route_scale / total * (gate[k] - mean_term) * score[k] * (1.0 - score[k])
        score_grad_ref[k : k + 1, :] = grad
        dense = jnp.where(named[k], grad, dense)
    sides = [jnp.where(odd, 0.0, dense).astype(BF16), jnp.where(odd, dense, 0.0).astype(BF16)]
    sides = jnp.concatenate(sides, axis=1)
    for side in range(2):
        columns = act_ref[:, side * half : (side + 1) * half]
        pair = jnp.concatenate([columns[:, :quarter], columns[:, quarter:]], axis=0)
        part_ref[side * rows : (side + 1) * rows, :] = jnp.dot(
            sides, pair, preferred_element_type=F32
        ).astype(BF16)


def input_kernel(ids_ref, score_grad_ref, got_ref, out_ref):
    rows = got_ref.shape[0]
    tokens, width = out_ref.shape
    half = width // 2
    named = named_rows(ids_ref[...], rows)
    odd = (iota((rows, tokens), 0) & 1) == 1
    dense = jnp.zeros((rows, tokens), F32)
    for k in range(2):
        dense = jnp.where(named[k], score_grad_ref[k : k + 1, :], dense)
    for h in range(2):
        picked = jnp.where(odd == (h == 1), dense, 0.0).astype(BF16)
        out_ref[:, h * half : (h + 1) * half] = lax.dot_general(
            picked, got_ref[:, width:], TN, preferred_element_type=F32
        ).astype(BF16)


def sum_kernel(got_ref, out_ref):
    rows, sources = out_ref.shape[0], got_ref.shape[0]
    pick = ones_where((iota((rows, sources), 0) & 7) == (iota((rows, sources), 1) & 7))
    out_ref[...] = jnp.dot(pick, got_ref[...], preferred_element_type=F32).astype(BF16)


def final_kernel(got_ref, out_ref):
    experts = out_ref.shape[0]
    sources, block = got_ref.shape
    row, col = iota((experts, sources), 0), iota((experts, sources), 1)
    for piece in range(4):
        pick = ones_where((col & 15) == ((piece >> 1) * 8 + row * 2 + (piece & 1)))
        out_ref[:, piece * block : (piece + 1) * block] = jnp.dot(
            pick, got_ref[...], preferred_element_type=F32
        )


def call(kernel, name, out_shape, *args, cost=None):
    return pl.pallas_call(
        kernel, out_shape=out_shape, compiler_params=BIG, cost_estimate=cost, name=name
    )(*args)


def body(activations, out_grad, router_weight, expert_ids, saved_output):
    experts, width = router_weight.shape
    tokens = activations.shape[0]
    planes = lax.axis_size("pairs") * lax.axis_size("side")
    rows = experts * saved_output.shape[2]
    ids = expert_ids.T
    packed = pack(saved_output.reshape(rows, width), router_weight)
    got = lax.all_to_all(packed, "expert", split_axis=0, concat_axis=0, tiled=True)
    score_grad, part = call(
        score_kernel,
        "scores",
        (
            jax.ShapeDtypeStruct((2, tokens), F32),
            jax.ShapeDtypeStruct((2 * rows, width // 4), BF16),
        ),
        ids,
        got,
        activations,
        out_grad,
    )
    part = lax.all_to_all(part, ("side", "expert"), split_axis=0, concat_axis=0, tiled=True)
    input_grad = call(
        input_kernel,
        "input_grads",
        jax.ShapeDtypeStruct((tokens, width), BF16),
        ids,
        score_grad,
        got,
        cost=pl.CostEstimate(
            flops=2 * tokens * rows * width, bytes_accessed=4 * tokens * width, transcendentals=0
        ),
    )
    summed = call(
        sum_kernel,
        "sum_planes",
        jax.ShapeDtypeStruct((planes * 2 * experts, width // 4), BF16),
        part,
    )
    summed = lax.all_to_all(summed, ("pairs", "side"), split_axis=0, concat_axis=0, tiled=True)
    router_grad = call(
        final_kernel, "sum_batches", jax.ShapeDtypeStruct((experts, width), F32), summed
    )
    return input_grad, score_grad.T, router_grad


def solution(mesh):
    dp, owners = mesh.shape["dp"], mesh.shape["expert"]
    mesh = Mesh(mesh.devices.reshape(dp // 2, 2, owners), ("pairs", "side", "expert"))
    tokens = P(("pairs", "side", "expert"), None)
    in_specs = (
        tokens,
        tokens,
        P("expert", None),
        tokens,
        P(("pairs", "side"), "expert", None, None),
    )
    out_specs = (tokens, tokens, P("expert", None))
    return jax.shard_map(body, mesh=mesh, in_specs=in_specs, out_specs=out_specs, check_vma=False)
```

time: 289 us -> 103 us (0.36)
  waiting for transfers between devices: 139 us -> 15.8 us
  blocking collectives: 97.2 us -> 63.1 us
  between operations: 14.8 us -> 0.7 us
  other arithmetic: 8.37 us -> 0 us
  Pallas kernels: 0 us -> 7.61 us
  local copies, waits for them, and re-layouts: 7.1 us -> 0.03 us
  matrix products: 5.19 us -> 0 us
    unnamed x2 -> x0, waiting for transfers between devices: 134 us -> none
    all_to_all x0 -> x2, blocking collectives: none -> 63.1 us  [the longest x1 41.9 us: body(): lax.all_to_all(packed, 'expert', split_axis=0, concat_axis=0, tiled=True)]
    psum x1 -> x0, blocking collectives: 57.5 us -> none  [body(): router_grad = lax.psum(local_rows, 'dp')]
    all_gather x1 -> x0, blocking collectives: 39.7 us -> none  [body(): router_full = lax.all_gather(router_weight, 'expert', axis=0, tiled=True)]
    all_to_all x2 -> x1, waiting for transfers between devices: 5.36 us -> 15.8 us  [body(): lax.all_to_all(summed, ('pairs', 'side'), split_axis=0, concat_axis=0, ti...]
    pallas_call x0 -> x5, Pallas kernels: none -> 7.61 us  [the longest x4 5.02 us: call(): pl.pallas_call(kernel, out_shape=out_shape, compiler_params=BIG, cost_est...]
    dot_general x4 -> x0, matrix products: 5.19 us -> none  [the longest x1 1.65 us: body(): lax.dot_general(dense, activations, (((0,), (0,)), ((), ())), preferred_e...]
    unnamed x1 -> x0, other arithmetic: 4.57 us -> none
  transfers between devices with their start and end apart: 3 -> 1, of which waited for: 2 -> 1; matrix products, arithmetic and copies ran while one was open for 2% -> 0% of each run, Pallas kernels for 0% -> 1%
where the time goes in v2:
time: 103 us; the launch traced here: 102 us
  blocking collectives  63.1 us (61%)
  waiting for transfers between devices  15.8 us (15%)
  starting transfers between devices  14.3 us (14%)
  Pallas kernels  7.61 us (7%)
    all_to_all x1, blocking collectives, body(): lax.all_to_all(packed, 'expert', split_axis=0, concat_axis=0, tiled=True)  41.9 us
    all_to_all x1, blocking collectives, body(): lax.all_to_all(part, ('side', 'expert'), split_axis=0, concat_axis=0, til...  21.2 us
    all_to_all x1, waiting for transfers between devices, body(): lax.all_to_all(summed, ('pairs', 'side'), split_axis=0, concat_axis=0, ti...  15.8 us
    all_to_all x1, starting transfers between devices, body(): lax.all_to_all(summed, ('pairs', 'side'), split_axis=0, concat_axis=0, ti...  14.3 us
    pallas_call x4, Pallas kernels, call(): pl.pallas_call(kernel, out_shape=out_shape, compiler_params=BIG, cost_est...  5.02 us
    pallas_call x1, Pallas kernels, pack(): pl.pallas_call(pack_kernel, in_specs=[pl.BlockSpec(memory_space=pltpu.HBM...  2.59 us
  transfers between devices with their start and end apart: 1, of which 1 were waited for; matrix products, arithmetic and copies ran while one was open for 0% of the time, Pallas kernels for 1%

profile of v2, /device:TPU:6, one launch (start us, length us, event | category | flops | bytes accessed | tf_op | source)
XLA Modules:
  0.0 101.5 jit_solution(5068924624871504079)
XLA Ops:
  0.6 2.6 %pack_rows.1 = bf16[256,5376]{1,0:T(8,128)(2,1)S(1)} custom-call(bf16[256,3584]{1,0:T(8,128)(2,1)} %bitcast.18, bf16[4,3584]{1,0:T(4,128)(2,1)} %weight_hbm.1), custom_call_target="tpu_custom_call" | custom-call | tf_op jit(solution)/shard_map/pack_rows/pallas_call | solution.py:50
  3.2 0.0 copy-start
  3.2 0.0 copy-start.1
  3.3 0.0 copy-start.2
  3.3 41.9 %all_to_all.33 = bf16[32,8,5376]{2,1,0:T(8,128)(2,1)S(1)} all-to-all(bf16[32,8,5376]{2,1,0:T(8,128)(2,1)S(1)} %bitcast.11), channel_id=1, replica_groups=mesh['pairs'=8,'side'=2,'expert'=32] {'expert'}, dimensions={0} | all-to-all | bytes 5505024 | tf_op jit(solution)/shard_map/all_to_all | solution.py:152
  45.2 0.0 copy-done
  45.2 0.0 copy-done.1
  45.2 0.0 copy-done.2
  45.2 1.8 %scores.1 = (f32[2,128]{1,0:T(2,128)}, bf16[512,896]{1,0:T(8,128)(2,1)S(1)}) custom-call(s32[2,128]{1,0:T(2,128)S(1)} %bitcast.15, bf16[256,5376]{1,0:T(8,128)(2,1)S(1)} %bitcast.9, bf16[128,3584]{1,0:T(8,128)(2,1)S(1)} %copy-done, bf16[128,3584]{1,0:T(8,128)(2,1)S(1)} %copy-done.1), custom_call_target="tpu_custom_call" | custom-call | tf_op jit(solution)/shard_map/scores/pallas_call | solution.py:140
  46.9 0.0 copy-start.3
  47.0 21.2 %all_to_all.34 = bf16[64,8,896]{2,1,0:T(8,128)(2,1)S(1)} all-to-all(bf16[64,8,896]{2,1,0:T(8,128)(2,1)S(1)} %bitcast.13), channel_id=1, replica_groups=mesh['pairs'=8,'side'=2,'expert'=32] {'side','expert'}, dimensions={0} | all-to-all | bytes 1835008 | tf_op jit(solution)/shard_map/all_to_all | solution.py:165
  68.2 1.0 sum_planes.1
  69.2 14.3 %all-to-all-start.2 = ((bf16[16,8,896]{2,1,0:T(8,128)(2,1)}), bf16[16,8,896]{2,1,0:T(8,128)(2,1)S(1)}, u32[]{:S(2)}, u32[]{:S(2)}) async-start(bf16[16,8,896]{2,1,0:T(8,128)(2,1)} %bitcast.7), calls=%async_computation.2 | async-start | bytes 458752 | tf_op jit(solution)/shard_map/all_to_all | solution.py:183
  83.5 0.0 copy-done.3
  83.5 1.4 %input_grads.1 = bf16[128,3584]{1,0:T(8,128)(2,1)} custom-call(s32[2,128]{1,0:T(2,128)S(1)} %bitcast.16, f32[2,128]{1,0:T(2,128)S(1)} %copy-done.3, bf16[256,5376]{1,0:T(8,128)(2,1)S(1)} %bitcast.10), custom_call_target="tpu_custom_call" | custom-call | flops 234881024 | bytes 1835008 | tf_op jit(solution)/shard_map/input_grads/pallas_call | solution.py:140
  84.9 15.8 %all-to-all-done.2 = bf16[16,8,896]{2,1,0:T(8,128)(2,1)S(1)} async-done(((bf16[16,8,896]{2,1,0:T(8,128)(2,1)}), bf16[16,8,896]{2,1,0:T(8,128)(2,1)S(1)}, u32[]{:S(2)}, u32[]{:S(2)}) %all-to-all-start.2) | async-done | bytes 229408 | tf_op jit(solution)/shard_map/all_to_all | solution.py:183
  100.7 0.9 sum_batches.1
Async XLA Ops:
  3.2 41.9 %copy-start = (bf16[128,3584]{1,0:T(8,128)(2,1)S(1)}, bf16[128,3584]{1,0:T(8,128)(2,1)}, u32[]{:S(2)}) copy-start(bf16[128,3584]{1,0:T(8,128)(2,1)} %act_ref.1) | copy-start | bytes 2752516
  3.2 41.9 %copy-start.1 = (bf16[128,3584]{1,0:T(8,128)(2,1)S(1)}, bf16[128,3584]{1,0:T(8,128)(2,1)}, u32[]{:S(2)}) copy-start(bf16[128,3584]{1,0:T(8,128)(2,1)} %grad_ref.1) | copy-start | bytes 2752516
  3.3 41.9 %copy-start.2 = (s32[128,2]{0,1:T(2,128)S(1)}, s32[128,2]{0,1:T(2,128)}, u32[]{:S(2)}) copy-start(s32[128,2]{0,1:T(2,128)} %param.8) | copy-start | bytes 3076
  46.9 36.5 %copy-start.3 = (f32[2,128]{1,0:T(2,128)S(1)}, f32[2,128]{1,0:T(2,128)}, u32[]{:S(2)}) copy-start(f32[2,128]{1,0:T(2,128)} %get-tuple-element.5.score_grad_ref) | copy-start | bytes 3076
  69.2 31.5 %all-to-all-start.2 = ((bf16[16,8,896]{2,1,0:T(8,128)(2,1)}), bf16[16,8,896]{2,1,0:T(8,128)(2,1)S(1)}, u32[]{:S(2)}, u32[]{:S(2)}) async-start(bf16[16,8,896]{2,1,0:T(8,128)(2,1)} %bitcast.7), calls=%async_computation.2 | async-start | bytes 458752 | tf_op jit(solution)/shard_map/all_to_all | solution.py:183

commit v3 on v2

v3 whole, which is shorter than its diff:
```python
import jax
import jax.numpy as jnp
from jax import lax
from jax.experimental import pallas as pl
from jax.experimental.pallas import tpu as pltpu
from jax.sharding import Mesh, PartitionSpec as P

route_scale = 2.5
BF16, F32 = jnp.bfloat16, jnp.float32
NT = (((1,), (1,)), ((), ()))
TN = (((0,), (0,)), ((), ()))
WIDE = 512
BIG = pltpu.CompilerParams(vmem_limit_bytes=40 * 1024 * 1024)


def iota(shape, dim):
    return lax.broadcasted_iota(jnp.int32, shape, dim)


def ones_where(mask):
    return jnp.where(mask, 1.0, 0.0).astype(BF16)


def pack_kernel(saved_hbm, weight_hbm, out_hbm, saved_ref, weight_ref, out_ref, in_sem, out_sem):
    rows, width = saved_ref.shape
    half, quarter, per_core = width // 2, width // 4, rows // 2
    halves = [slice(k * half, (k + 1) * half) for k in range(2)]
    copies = [
        pltpu.make_async_copy(saved_hbm.at[:, block], saved_ref.at[:, block], in_sem.at[k])
        for k, block in enumerate(halves)
    ]
    copies.append(pltpu.make_async_copy(weight_hbm, weight_ref, in_sem.at[2]))
    for copy in copies:
        copy.start()
    row, col = iota((rows, rows), 0), iota((rows, rows), 1)
    local = row & (per_core - 1)
    source = ((local >> 1) & 3) * (rows // 4) + (local >> 3) * 4 + (local & 1)
    pick = ones_where(col == source + jnp.where(row < per_core, 0, 2))
    row, col = iota((per_core, 8), 0), iota((per_core, 8), 1)
    pick_weight = ones_where(col == ((row >> 1) & 3) + (row & 1) * 4)
    copies[2].wait()
    sent = []
    for k, block in enumerate(halves):
        mine = slice(k * per_core, (k + 1) * per_core)
        parts = [
            weight_ref[:, k * half + m * quarter : k * half + (m + 1) * quarter] for m in range(2)
        ]
        out_ref[mine, width:] = jnp.dot(
            pick_weight, jnp.concatenate(parts, axis=0), preferred_element_type=F32
        ).astype(BF16)
        copies[k].wait()
        out = jnp.dot(pick, saved_ref[:, block], preferred_element_type=F32).astype(BF16)
        for core in range(2):
            out_ref[mine, halves[core]] = out[core * per_core : (core + 1) * per_core]
        sent.append(pltpu.make_async_copy(out_ref.at[mine], out_hbm.at[mine], out_sem.at[k]))
        sent[k].start()
    for copy in sent:
        copy.wait()


def pack(saved, weight):
    rows, width = saved.shape
    packed = (rows, width + width // 4)
    return pl.pallas_call(
        pack_kernel,
        in_specs=[pl.BlockSpec(memory_space=pltpu.HBM)] * 2,
        out_specs=pl.BlockSpec(memory_space=pltpu.HBM),
        out_shape=pltpu.HBM(packed, BF16),
        scratch_shapes=[
            pltpu.VMEM((rows, width), BF16),
            pltpu.VMEM(weight.shape, BF16),
            pltpu.VMEM(packed, BF16),
            pltpu.SemaphoreType.DMA((3,)),
            pltpu.SemaphoreType.DMA((2,)),
        ],
        compiler_params=BIG,
        name="pack_rows",
    )(in_hbm(saved), in_hbm(weight))


def in_hbm(array):
    return pltpu.with_memory_space_constraint(array, pltpu.HBM)


def half_copies(core, act_hbm, grad_hbm, out_ref, sem):
    tokens, half = act_hbm.shape[0], act_hbm.shape[1] // 2
    block = pl.ds(pl.multiple_of(core * half, 128), half)
    return [
        pltpu.make_async_copy(
            array.at[:, block], out_ref.at[pl.ds(i * tokens, tokens)], sem.at[i]
        )
        for i, array in enumerate((act_hbm, grad_hbm))
    ]


def halves_kernel(core_ref, act_hbm, grad_hbm, out_ref, sem):
    copies = half_copies(1 - core_ref[0], act_hbm, grad_hbm, out_ref, sem)
    for copy in copies:
        copy.start()
    for copy in copies:
        copy.wait()


def halves_for_other(core, act, grad):
    tokens, width = act.shape
    return pl.pallas_call(
        halves_kernel,
        in_specs=[pl.BlockSpec(memory_space=pltpu.SMEM)]
        + [pl.BlockSpec(memory_space=pltpu.HBM)] * 2,
        out_shape=jax.ShapeDtypeStruct((2 * tokens, width // 2), BF16),
        scratch_shapes=[pltpu.SemaphoreType.DMA((2,))],
        compiler_params=BIG,
        name="halves_for_other",
    )(core, in_hbm(act), in_hbm(grad))


def named_rows(ids, rows):
    row = iota((rows, ids.shape[1]), 0)
    chips = rows // 16
    expert = ((row >> 3) & (chips - 1)) * 8 + (row >= rows // 2) * 4 + ((row >> 1) & 3)
    return [expert == ids[k : k + 1, :] for k in range(2)]


def odd_rows(rows, tokens):
    return (iota((rows, tokens), 0) & 1) == 1


def dots_kernel(
    core_ref, ids_ref, other_ids_ref, other_ref, got_ref, act_hbm, grad_hbm, out_ref, own_ref, sem
):
    rows = got_ref.shape[0]
    tokens, half = own_ref.shape[0] // 2, own_ref.shape[1]
    quarter = half // 2
    core = core_ref[0]
    copies = half_copies(core, act_hbm, grad_hbm, own_ref, sem)
    for copy in copies:
        copy.start()
    odd = odd_rows(rows, tokens)
    before = ones_where(iota((tokens, tokens), 0) < iota((tokens, tokens), 1))
    for owner, ids, halves_ref in (
        (1 - core, other_ids_ref[...], other_ref),
        (core, ids_ref[...], own_ref),
    ):
        if halves_ref is own_ref:
            for copy in copies:
                copy.wait()
        saved = got_ref[:, pl.ds(pl.multiple_of(owner * half, 128), half)]
        dots = lax.dot_general(
            saved, halves_ref[tokens:, :], NT, preferred_element_type=F32
        )
        named = named_rows(ids, rows)
        earlier = jnp.dot(ones_where(named[0] | named[1]), before, preferred_element_type=F32)
        dots = jnp.where(earlier == jnp.where(odd, 1.0, 0.0), dots, 0.0)
        parts = [halves_ref[:tokens, :quarter], halves_ref[:tokens, quarter:]]
        logits = lax.dot_general(
            got_ref[:, 2 * half :],
            jnp.concatenate(parts, axis=0),
            NT,
            preferred_element_type=F32,
        )
        logits = jnp.where(odd, logits[:, tokens:], logits[:, :tokens])
        sums = [
            jnp.sum(jnp.where(named[k], values, 0.0), axis=0, keepdims=True)
            for values in (dots, logits)
            for k in range(2)
        ]
        sums.append(jnp.zeros((4, tokens), F32))
        out_ref[pl.ds(pl.multiple_of(owner * 8, 8), 8), :] = jnp.concatenate(sums, axis=0)


def gate_dots(core, ids, other_ids, other, got, act, grad):
    tokens = act.shape[0]
    vmem, hbm = pl.BlockSpec(memory_space=pltpu.VMEM), pl.BlockSpec(memory_space=pltpu.HBM)
    return pl.pallas_call(
        dots_kernel,
        in_specs=[pl.BlockSpec(memory_space=pltpu.SMEM)] + [vmem] * 4 + [hbm] * 2,
        out_shape=(
            jax.ShapeDtypeStruct((16, tokens), F32),
            jax.ShapeDtypeStruct(other.shape, BF16),
        ),
        scratch_shapes=[pltpu.SemaphoreType.DMA((2,))],
        compiler_params=BIG,
        name="gate_dots",
    )(core, ids, other_ids, other, got, in_hbm(act), in_hbm(grad))


def score_kernel(
    core_ref, mine_ref, theirs_ref, ids_ref, other_ids_ref, own_ref, other_ref, *outs
):
    score_grad_ref, part_ref = outs
    rows, wide = part_ref.shape[0] // 2, part_ref.shape[1]
    tokens, quarter = own_ref.shape[0] // 2, own_ref.shape[1] // 2
    core = core_ref[0]
    odd = odd_rows(rows, tokens)
    left = []
    for owner, ids in ((core, ids_ref[...]), (1 - core, other_ids_ref[...])):
        block = pl.ds(pl.multiple_of(owner * 8, 8), 8)
        sums = mine_ref[block, :] + theirs_ref[block, :]
        gate = [sums[k : k + 1, :] for k in range(2)]
        score = [jax.nn.sigmoid(sums[2 + k : 3 + k, :]) for k in range(2)]
        total = score[0] + score[1]
        mean_term = (score[0] * gate[0] + score[1] * gate[1]) / total
        named = named_rows(ids, rows)
        dense = jnp.zeros((rows, tokens), F32)
        for k in range(2):
            grad = route_scale / total * (gate[k] - mean_term) * score[k] * (1.0 - score[k])
            if not left:
                score_grad_ref[k : k + 1, :] = grad
            dense = jnp.where(named[k], grad, dense)
        left += [jnp.where(odd, 0.0, dense).astype(BF16), jnp.where(odd, dense, 0.0).astype(BF16)]
    left = jnp.concatenate(left, axis=1)
    rest = jnp.zeros((tokens, 2 * wide - quarter), BF16)
    for side in range(2):
        right = []
        for halves_ref in (own_ref, other_ref):
            act = halves_ref[:tokens, side * quarter : (side + 1) * quarter]
            right += [act[:, :wide], jnp.concatenate([act[:, wide:], rest], axis=1)]
        part_ref[side * rows : (side + 1) * rows, :] = jnp.dot(
            left, jnp.concatenate(right, axis=0), preferred_element_type=F32
        ).astype(BF16)


def input_kernel(core_ref, ids_ref, score_grad_ref, own_ref, other_ref, out_ref):
    rows, quarter = own_ref.shape
    tokens = out_ref.shape[0]
    odd = odd_rows(rows, tokens)
    named = named_rows(ids_ref[...], rows)
    dense = jnp.zeros((rows, tokens), F32)
    for k in range(2):
        dense = jnp.where(named[k], score_grad_ref[k : k + 1, :], dense)
    for m in range(2):
        picked = jnp.where(odd == (m == 1), dense, 0.0).astype(BF16)
        for core, weight_ref in ((core_ref[0], own_ref), (1 - core_ref[0], other_ref)):
            block = pl.ds(pl.multiple_of((core * 2 + m) * quarter, 128), quarter)
            out_ref[:, block] = lax.dot_general(
                picked, weight_ref[...], TN, preferred_element_type=F32
            ).astype(BF16)


def sum_kernel(got_ref, out_ref):
    rows, sources = out_ref.shape[0], got_ref.shape[0]
    wide, columns = got_ref.shape[1], out_ref.shape[1]
    row, col = iota((rows, sources), 0), iota((rows, sources), 1)
    sent_by = (col & (sources // 2 - 1)) >= sources // 4
    same = (row & 7) == jnp.where(sent_by, 4, 0) + ((col >> 1) & 3)
    for h in range(2):
        pick = ones_where(same & ((col & 1) == h))
        start = h * wide
        count = wide if h == 0 else columns - wide
        out_ref[:, start : start + count] = jnp.dot(
            pick, got_ref[:, :count], preferred_element_type=F32
        ).astype(BF16)


def final_kernel(got_ref, out_ref):
    experts = out_ref.shape[0]
    sources, quarter = got_ref.shape
    row, col = iota((experts, sources), 0), iota((experts, sources), 1)
    for half in range(2):
        for side in range(2):
            pick = ones_where((col & 15) == side * 8 + half * 4 + row)
            start = (half * 2 + side) * quarter
            out_ref[:, start : start + quarter] = jnp.dot(
                pick, got_ref[...], preferred_element_type=F32
            )


def call(kernel, name, out_shape, *args, cost=None):
    return pl.pallas_call(
        kernel,
        in_specs=[
            pl.BlockSpec(memory_space=pltpu.SMEM if a.shape == (1,) else pltpu.VMEM) for a in args
        ],
        out_shape=out_shape,
        compiler_params=BIG,
        cost_estimate=cost,
        name=name,
    )(*args)


def body(activations, out_grad, router_weight, expert_ids, saved_output):
    experts, width = router_weight.shape
    tokens = activations.shape[0]
    planes = lax.axis_size("pairs") * lax.axis_size("side")
    rows = experts * saved_output.shape[2]
    core = lax.axis_index("core").astype(jnp.int32).reshape(1)
    ids = expert_ids.T

    def swap(x):
        return lax.ppermute(x, "core", [(0, 1), (1, 0)])

    packed = pack(saved_output.reshape(rows, width), router_weight)
    got = lax.all_to_all(packed, ("core", "chip"), split_axis=0, concat_axis=0, tiled=True)
    other = swap(halves_for_other(core, activations, out_grad))
    other_ids = swap(ids)
    mine, own = gate_dots(core, ids, other_ids, other, got, activations, out_grad)
    score_grad, part = call(
        score_kernel,
        "scores",
        (
            jax.ShapeDtypeStruct((2, tokens), F32),
            jax.ShapeDtypeStruct((2 * rows, WIDE), BF16),
        ),
        core,
        mine,
        swap(mine),
        ids,
        other_ids,
        own,
        other,
    )
    part = lax.all_to_all(
        part, ("side", "core", "chip"), split_axis=0, concat_axis=0, tiled=True
    )
    summed = call(
        sum_kernel,
        "sum_owners",
        jax.ShapeDtypeStruct((planes * 2 * experts, width // 4), BF16),
        part,
    )
    got, summed = lax.optimization_barrier((got, summed))
    weight = got[:, width:]
    input_grad = call(
        input_kernel,
        "input_grads",
        jax.ShapeDtypeStruct((tokens, width), BF16),
        core,
        ids,
        score_grad,
        weight,
        swap(weight),
        cost=pl.CostEstimate(
            flops=2 * tokens * rows * width, bytes_accessed=4 * tokens * width, transcendentals=0
        ),
    )
    summed = lax.all_to_all(summed, ("pairs", "side"), split_axis=0, concat_axis=0, tiled=True)
    router_grad = call(
        final_kernel, "sum_batches", jax.ShapeDtypeStruct((experts, width), F32), summed
    )
    return input_grad, score_grad.T, router_grad


def solution(mesh):
    dp, owners = mesh.shape["dp"], mesh.shape["expert"]
    devices = mesh.devices.reshape(dp // 2, 2, owners // 2, 2)
    mesh = Mesh(devices, ("pairs", "side", "chip", "core"))
    tokens = P(("pairs", "side", "chip", "core"), None)
    in_specs = (
        tokens,
        tokens,
        P(("chip", "core"), None),
        tokens,
        P(("pairs", "side"), ("chip", "core"), None, None),
    )
    out_specs = (tokens, tokens, P(("chip", "core"), None))
    return jax.shard_map(body, mesh=mesh, in_specs=in_specs, out_specs=out_specs, check_vma=False)
```

time: 103 us -> 99.9 us (0.970)
  blocking collectives: 63.1 us -> 15.8 us
  waiting for transfers between devices: 15.8 us -> 39.6 us
  starting transfers between devices: 14.3 us -> 31.3 us
  Pallas kernels: 7.61 us -> 10.5 us
    all_to_all x2 -> x1, blocking collectives: 63.1 us -> 15.8 us  [body(): lax.all_to_all(part, ('side', 'core', 'chip'), split_axis=0, concat_axis=...]
    all_to_all x0 -> x1, waiting for transfers between devices: none -> 23.9 us  [body(): lax.all_to_all(packed, ('core', 'chip'), split_axis=0, concat_axis=0, til...]
    all_to_all x0 -> x1, starting transfers between devices: none -> 9.58 us  [body(): lax.all_to_all(packed, ('core', 'chip'), split_axis=0, concat_axis=0, til...]
    ppermute x0 -> x4, starting transfers between devices: none -> 8.21 us  [swap(): return lax.ppermute(x, 'core', [(0, 1), (1, 0)])]
    all_to_all x1, waiting for transfers between devices: 15.8 us -> 12 us  [body(): lax.all_to_all(summed, ('pairs', 'side'), split_axis=0, concat_axis=0, ti...]
    ppermute x0 -> x4, waiting for transfers between devices: none -> 3.71 us  [swap(): return lax.ppermute(x, 'core', [(0, 1), (1, 0)])]
    pallas_call x4 -> x6, Pallas kernels: 5.02 us -> 7.01 us  [the longest x4 4 us: call(): pl.pallas_call(kernel, in_specs=[pl.BlockSpec(memory_space=pltpu.SMEM if...]
  transfers between devices with their start and end apart: 1 -> 6, of which waited for: 1 -> 5; matrix products, arithmetic and copies ran while one was open for 0% -> 0% of each run, Pallas kernels for 1% -> 3%
where the time goes in v3:
time: 99.9 us; the launch traced here: 98 us
  waiting for transfers between devices  39.6 us (40%)
  starting transfers between devices  31.3 us (31%)
  blocking collectives  15.8 us (16%)
  Pallas kernels  10.5 us (11%)
    all_to_all x1, waiting for transfers between devices, body(): lax.all_to_all(packed, ('core', 'chip'), split_axis=0, concat_axis=0, til...  23.9 us
    all_to_all x1, blocking collectives, body(): lax.all_to_all(part, ('side', 'core', 'chip'), split_axis=0, concat_axis=...  15.8 us
    all_to_all x1, starting transfers between devices, body(): lax.all_to_all(summed, ('pairs', 'side'), split_axis=0, concat_axis=0, ti...  13.5 us
    all_to_all x1, waiting for transfers between devices, body(): lax.all_to_all(summed, ('pairs', 'side'), split_axis=0, concat_axis=0, ti...  12 us
    all_to_all x1, starting transfers between devices, body(): lax.all_to_all(packed, ('core', 'chip'), split_axis=0, concat_axis=0, til...  9.58 us
    ppermute x4, starting transfers between devices, swap(): return lax.ppermute(x, 'core', [(0, 1), (1, 0)])  8.21 us
    pallas_call x4, Pallas kernels, call(): pl.pallas_call(kernel, in_specs=[pl.BlockSpec(memory_space=pltpu.SMEM if...  4 us
    ppermute x4, waiting for transfers between devices, swap(): return lax.ppermute(x, 'core', [(0, 1), (1, 0)])  3.71 us
  transfers between devices with their start and end apart: 6, of which 5 were waited for; matrix products, arithmetic and copies ran while one was open for 0% of the time, Pallas kernels for 3%

profile of v3, /device:TPU:6, one launch (start us, length us, event | category | flops | bytes accessed | tf_op | source)
XLA Modules:
  0.0 98.0 jit_solution(13922001542250675762)
XLA Ops:
  0.6 3.5 %pack_rows.1 = bf16[256,4480]{1,0:T(8,128)(2,1)} custom-call(bf16[256,3584]{1,0:T(8,128)(2,1)} %bitcast.21, bf16[4,3584]{1,0:T(4,128)(2,1)} %weight_hbm.1), custom_call_target="tpu_custom_call" | custom-call | tf_op jit(solution)/shard_map/pack_rows/pallas_call | solution.py:64
  4.1 9.6 %all-to-all-start = ((bf16[32,8,4480]{2,1,0:T(8,128)(2,1)}), bf16[32,8,4480]{2,1,0:T(8,128)(2,1)S(1)}, u32[]{:S(2)}, u32[]{:S(2)}) async-start(bf16[32,8,4480]{2,1,0:T(8,128)(2,1)} %bitcast.20), calls=%async_computation | async-start | bytes 4587520 | tf_op jit(solution)/shard_map/all_to_all | solution.py:293
  13.7 0.0 copy-start
  13.7 1.2 %halves_for_other.1 = bf16[256,1792]{1,0:T(8,128)(2,1)S(1)} custom-call(s32[1]{0:T(128)} %bitcast.core_ref, bf16[128,3584]{1,0:T(8,128)(2,1)} %act_hbm.3, bf16[128,3584]{1,0:T(8,128)(2,1)} %grad_hbm.3), custom_call_target="tpu_custom_call" | custom-call | tf_op jit(solution)/shard_map/halves_for_other/pallas_call | solution.py:106
  14.9 2.1 %collective-permute-start.1 = (bf16[256,1792]{1,0:T(8,128)(2,1)S(1)}, bf16[256,1792]{1,0:T(8,128)(2,1)S(1)}, u32[]{:S(2)}, u32[]{:S(2)}) collective-permute-start(bf16[256,1792]{1,0:T(8,128)(2,1)S(1)} %halves_for_other.1), channel_id=1, source_target_pairs={{0,1},{1,0},{2,3},{3,2},{4,5},{5,4},{6,7},{7,6},{8,9},{9,8},{10,11... | collective-permute-start | bytes 2752520 | tf_op jit(solution)/shard_map/ppermute | solution.py:290
  17.1 0.0 copy-done
  17.1 2.2 %collective-permute-start = (s32[2,128]{1,0:T(2,128)S(1)}, s32[2,128]{1,0:T(2,128)S(1)}, u32[]{:S(2)}, u32[]{:S(2)}) collective-permute-start(s32[2,128]{1,0:T(2,128)S(1)} %bitcast.15), channel_id=1, source_target_pairs={{0,1},{1,0},{2,3},{3,2},{4,5},{5,4},{6,7},{7,6},{8,9},{9,8},{10,11... | collective-permute-start | bytes 3080 | tf_op jit(solution)/shard_map/ppermute | solution.py:290
  19.3 0.8 collective-permute-done.other_ids_ref
  20.1 0.0 collective-permute-done.1.other_ref
  20.1 23.9 %all-to-all-done = bf16[32,8,4480]{2,1,0:T(8,128)(2,1)S(1)} async-done(((bf16[32,8,4480]{2,1,0:T(8,128)(2,1)}), bf16[32,8,4480]{2,1,0:T(8,128)(2,1)S(1)}, u32[]{:S(2)}, u32[]{:S(2)}) %all-to-all-start) | async-done | bytes 2293792 | tf_op jit(solution)/shard_map/all_to_all | solution.py:293
  44.0 1.8 %gate_dots.1 = (f32[16,128]{1,0:T(8,128)S(1)}, bf16[256,1792]{1,0:T(8,128)(2,1)S(1)}) custom-call(s32[1]{0:T(128)} %bitcast.core_ref, s32[2,128]{1,0:T(2,128)S(1)} %bitcast.16, s32[2,128]{1,0:T(2,128)S(1)} %collective-permute-done.other_ids_ref, bf16[256,1792]{1,0:T(8,128)(2,1)S(1)} %collective-permute-done.1.other_ref, bf16[256,4480]{1,0:T(8,128)(2,1)S(1)} %bitcast.10, ...), custom_call_target="tpu_custom_call" | custom-call | tf_op jit(solution)/shard_map/gate_dots/pallas_call | solution.py:174
  45.8 1.9 %collective-permute-start.2 = (f32[16,128]{1,0:T(8,128)S(1)}, f32[16,128]{1,0:T(8,128)S(1)}, u32[]{:S(2)}, u32[]{:S(2)}) collective-permute-start(f32[16,128]{1,0:T(8,128)S(1)} %get-tuple-element.9.mine_ref), channel_id=1, source_target_pairs={{0,1},{1,0},{2,3},{3,2},{4,5},{5,4},{6,7},{7,6},{8,9},{9,8},{10,11... | collective-permute-start | bytes 24584 | tf_op jit(solution)/shard_map/ppermute | solution.py:290
  47.7 1.1 %collective-permute-done.2.theirs_ref = f32[16,128]{1,0:T(8,128)S(1)} collective-permute-done((f32[16,128]{1,0:T(8,128)S(1)}, f32[16,128]{1,0:T(8,128)S(1)}, u32[]{:S(2)}, u32[]{:S(2)}) %collective-permute-start.2) | collective-permute-done | bytes 8224 | tf_op jit(solution)/shard_map/ppermute | solution.py:290
  48.9 0.7 scores.1
  49.6 0.0 copy-start.1
  49.6 15.8 %all_to_all.33 = bf16[64,8,512]{2,1,0:T(8,128)(2,1)S(1)} all-to-all(bf16[64,8,512]{2,1,0:T(8,128)(2,1)S(1)} %bitcast.14), channel_id=1, replica_groups=mesh['pairs'=8,'side'=2,'chip'=16,'core'=2] {'side','core','chip'}, dimensions={0} | all-to-all | bytes 1048576 | tf_op jit(solution)/shard_map/all_to_all | solution.py:312
  65.4 1.0 %sum_owners.1 = bf16[128,896]{1,0:T(8,128)(2,1)} custom-call(bf16[512,512]{1,0:T(8,128)(2,1)S(1)} %bitcast.12), custom_call_target="tpu_custom_call" | custom-call | tf_op jit(solution)/shard_map/sum_owners/pallas_call | solution.py:269
  66.4 13.5 %all-to-all-start.2 = ((bf16[16,8,896]{2,1,0:T(8,128)(2,1)}), bf16[16,8,896]{2,1,0:T(8,128)(2,1)S(1)}, u32[]{:S(2)}, u32[]{:S(2)}) async-start(bf16[16,8,896]{2,1,0:T(8,128)(2,1)} %bitcast.8), calls=%async_computation.2 | async-start | bytes 458752 | tf_op jit(solution)/shard_map/all_to_all | solution.py:336
  79.9 2.0 %collective-permute-start.3 = (bf16[256,896]{1,0:T(8,128)(2,1)S(1)}, bf16[256,896]{1,0:T(8,128)(2,1)S(1)}, u32[]{:S(2)}, u32[]{:S(2)}) collective-permute-start(bf16[256,896]{1,0:T(8,128)(2,1)S(1)} %slice.3.own_ref), channel_id=1, source_target_pairs={{0,1},{1,0},{2,3},{3,2},{4,5},{5,4},{6,7},{7,6},{8,9},{9,8},{10,11... | collective-permute-start | bytes 1376264 | tf_op jit(solution)/shard_map/ppermute | solution.py:290
  81.9 1.7 %collective-permute-done.3.other_ref = bf16[256,896]{1,0:T(8,128)(2,1)S(1)} collective-permute-done((bf16[256,896]{1,0:T(8,128)(2,1)S(1)}, bf16[256,896]{1,0:T(8,128)(2,1)S(1)}, u32[]{:S(2)}, u32[]{:S(2)}) %collective-permute-start.3) | collective-permute-done | bytes 458784 | tf_op jit(solution)/shard_map/ppermute | solution.py:290
  83.7 0.0 copy-done.1
  83.7 1.4 %input_grads.1 = bf16[128,3584]{1,0:T(8,128)(2,1)} custom-call(s32[1]{0:T(128)} %bitcast.core_ref, s32[2,128]{1,0:T(2,128)S(1)} %bitcast.18, f32[2,128]{1,0:T(2,128)S(1)} %copy-done.1, bf16[256,896]{1,0:T(8,128)(2,1)S(1)} %slice.3.own_ref, bf16[256,896]{1,0:T(8,128)(2,1)S(1)} %collective-permute-done.3.other_ref), custom_call_target="tpu_custom_call" | custom-call | flops 234881024 | bytes 1835008 | tf_op jit(solution)/shard_map/input_grads/pallas_call | solution.py:269
  85.1 12.0 %all-to-all-done.2 = bf16[16,8,896]{2,1,0:T(8,128)(2,1)S(1)} async-done(((bf16[16,8,896]{2,1,0:T(8,128)(2,1)}), bf16[16,8,896]{2,1,0:T(8,128)(2,1)S(1)}, u32[]{:S(2)}, u32[]{:S(2)}) %all-to-all-start.2) | async-done | bytes 229408 | tf_op jit(solution)/shard_map/all_to_all | solution.py:336
  97.1 0.9 sum_batches.1
  (1 shorter events, 0.0 us)
Async XLA Ops:
  4.1 39.8 %all-to-all-start = ((bf16[32,8,4480]{2,1,0:T(8,128)(2,1)}), bf16[32,8,4480]{2,1,0:T(8,128)(2,1)S(1)}, u32[]{:S(2)}, u32[]{:S(2)}) async-start(bf16[32,8,4480]{2,1,0:T(8,128)(2,1)} %bitcast.20), calls=%async_computation | async-start | bytes 4587520 | tf_op jit(solution)/shard_map/all_to_all | solution.py:293
  13.7 3.3 %copy-start = (s32[128,2]{0,1:T(2,128)S(1)}, s32[128,2]{0,1:T(2,128)}, u32[]{:S(2)}) copy-start(s32[128,2]{0,1:T(2,128)} %param.8) | copy-start | bytes 3076
  14.9 5.2 %collective-permute-start.1 = (bf16[256,1792]{1,0:T(8,128)(2,1)S(1)}, bf16[256,1792]{1,0:T(8,128)(2,1)S(1)}, u32[]{:S(2)}, u32[]{:S(2)}) collective-permute-start(bf16[256,1792]{1,0:T(8,128)(2,1)S(1)} %halves_for_other.1), channel_id=1, source_target_pairs={{0,1},{1,0},{2,3},{3,2},{4,5},{5,4},{6,7},{7,6},{8,9},{9,8},{10,11... | collective-permute-start | bytes 2752520 | tf_op jit(solution)/shard_map/ppermute | solution.py:290
  17.1 3.0 %collective-permute-start = (s32[2,128]{1,0:T(2,128)S(1)}, s32[2,128]{1,0:T(2,128)S(1)}, u32[]{:S(2)}, u32[]{:S(2)}) collective-permute-start(s32[2,128]{1,0:T(2,128)S(1)} %bitcast.15), channel_id=1, source_target_pairs={{0,1},{1,0},{2,3},{3,2},{4,5},{5,4},{6,7},{7,6},{8,9},{9,8},{10,11... | collective-permute-start | bytes 3080 | tf_op jit(solution)/shard_map/ppermute | solution.py:290
  45.8 3.1 %collective-permute-start.2 = (f32[16,128]{1,0:T(8,128)S(1)}, f32[16,128]{1,0:T(8,128)S(1)}, u32[]{:S(2)}, u32[]{:S(2)}) collective-permute-start(f32[16,128]{1,0:T(8,128)S(1)} %get-tuple-element.9.mine_ref), channel_id=1, source_target_pairs={{0,1},{1,0},{2,3},{3,2},{4,5},{5,4},{6,7},{7,6},{8,9},{9,8},{10,11... | collective-permute-start | bytes 24584 | tf_op jit(solution)/shard_map/ppermute | solution.py:290
  49.6 34.1 %copy-start.1 = (f32[2,128]{1,0:T(2,128)S(1)}, f32[2,128]{1,0:T(2,128)}, u32[]{:S(2)}) copy-start(f32[2,128]{1,0:T(2,128)} %get-tuple-element.11.score_grad_ref) | copy-start | bytes 3076
  66.4 30.8 %all-to-all-start.2 = ((bf16[16,8,896]{2,1,0:T(8,128)(2,1)}), bf16[16,8,896]{2,1,0:T(8,128)(2,1)S(1)}, u32[]{:S(2)}, u32[]{:S(2)}) async-start(bf16[16,8,896]{2,1,0:T(8,128)(2,1)} %bitcast.8), calls=%async_computation.2 | async-start | bytes 458752 | tf_op jit(solution)/shard_map/all_to_all | solution.py:336
  79.9 3.7 %collective-permute-start.3 = (bf16[256,896]{1,0:T(8,128)(2,1)S(1)}, bf16[256,896]{1,0:T(8,128)(2,1)S(1)}, u32[]{:S(2)}, u32[]{:S(2)}) collective-permute-start(bf16[256,896]{1,0:T(8,128)(2,1)S(1)} %slice.3.own_ref), channel_id=1, source_target_pairs={{0,1},{1,0},{2,3},{3,2},{4,5},{5,4},{6,7},{7,6},{8,9},{9,8},{10,11... | collective-permute-start | bytes 1376264 | tf_op jit(solution)/shard_map/ppermute | solution.py:290

commit v4 on v3

--- a/solution.py
+++ b/solution.py
@@ -9,7 +9,6 @@
 BF16, F32 = jnp.bfloat16, jnp.float32
 NT = (((1,), (1,)), ((), ()))
 TN = (((0,), (0,)), ((), ()))
-WIDE = 512
 BIG = pltpu.CompilerParams(vmem_limit_bytes=40 * 1024 * 1024)
 
 
@@ -30,8 +29,8 @@
         for k, block in enumerate(halves)
     ]
     copies.append(pltpu.make_async_copy(weight_hbm, weight_ref, in_sem.at[2]))
-    for copy in copies:
-        copy.start()
+    for i in (0, 2, 1):
+        copies[i].start()
     row, col = iota((rows, rows), 0), iota((rows, rows), 1)
     local = row & (per_core - 1)
     source = ((local >> 1) & 3) * (rows // 4) + (local >> 3) * 4 + (local & 1)
@@ -82,19 +81,26 @@
     return pltpu.with_memory_space_constraint(array, pltpu.HBM)
 
 
-def half_copies(core, act_hbm, grad_hbm, out_ref, sem):
-    tokens, half = act_hbm.shape[0], act_hbm.shape[1] // 2
-    block = pl.ds(pl.multiple_of(core * half, 128), half)
-    return [
-        pltpu.make_async_copy(
-            array.at[:, block], out_ref.at[pl.ds(i * tokens, tokens)], sem.at[i]
-        )
-        for i, array in enumerate((act_hbm, grad_hbm))
-    ]
-
-
-def halves_kernel(core_ref, act_hbm, grad_hbm, out_ref, sem):
-    copies = half_copies(1 - core_ref[0], act_hbm, grad_hbm, out_ref, sem)
+def half_copies(pieces, sems):
+    copies = []
+    for i, (array, half, out_ref) in enumerate(pieces):
+        width = out_ref.shape[1]
+        block = pl.ds(pl.multiple_of(half * width, 128), width)
+        copies.append(pltpu.make_async_copy(array.at[:, block], out_ref, sems.at[i]))
+    return copies
+
+
+def halves_kernel(core_ref, act_hbm, grad_hbm, out_ref, rest_ref, sem):
+    tokens = act_hbm.shape[0]
+    mine, theirs = core_ref[0], 1 - core_ref[0]
+    copies = half_copies(
+        [
+            (act_hbm, theirs, out_ref.at[pl.ds(0, tokens)]),
+            (grad_hbm, theirs, out_ref.at[pl.ds(tokens, tokens)]),
+            (act_hbm, mine, rest_ref),
+        ],
+        sem,
+    )
     for copy in copies:
         copy.start()
     for copy in copies:
@@ -107,8 +113,11 @@
         halves_kernel,
         in_specs=[pl.BlockSpec(memory_space=pltpu.SMEM)]
         + [pl.BlockSpec(memory_space=pltpu.HBM)] * 2,
-        out_shape=jax.ShapeDtypeStruct((2 * tokens, width // 2), BF16),
-        scratch_shapes=[pltpu.SemaphoreType.DMA((2,))],
+        out_shape=(
+            jax.ShapeDtypeStruct((2 * tokens, width // 2), BF16),
+            jax.ShapeDtypeStruct((tokens, width // 2), BF16),
+        ),
+        scratch_shapes=[pltpu.SemaphoreType.DMA((3,))],
         compiler_params=BIG,
         name="halves_for_other",
     )(core, in_hbm(act), in_hbm(grad))
@@ -126,13 +135,33 @@
 
 
 def dots_kernel(
-    core_ref, ids_ref, other_ids_ref, other_ref, got_ref, act_hbm, grad_hbm, out_ref, own_ref, sem
+    core_ref,
+    ids_ref,
+    other_ids_ref,
+    other_ref,
+    got_ref,
+    other_rest_hbm,
+    act_hbm,
+    grad_hbm,
+    out_ref,
+    own_ref,
+    rest_ref,
+    sem,
 ):
     rows = got_ref.shape[0]
     tokens, half = own_ref.shape[0] // 2, own_ref.shape[1]
     quarter = half // 2
     core = core_ref[0]
-    copies = half_copies(core, act_hbm, grad_hbm, own_ref, sem)
+    low, high = pl.ds(0, tokens), pl.ds(tokens, tokens)
+    copies = half_copies(
+        [
+            (act_hbm, core, own_ref.at[low]),
+            (grad_hbm, core, own_ref.at[high]),
+            (act_hbm, 1 - core, rest_ref.at[low]),
+            (other_rest_hbm, 0, rest_ref.at[high]),
+        ],
+        sem,
+    )
     for copy in copies:
         copy.start()
     odd = odd_rows(rows, tokens)
@@ -142,7 +171,7 @@
         (core, ids_ref[...], own_ref),
     ):
         if halves_ref is own_ref:
-            for copy in copies:
+            for copy in copies[:2]:
                 copy.wait()
         saved = got_ref[:, pl.ds(pl.multiple_of(owner * half, 128), half)]
         dots = lax.dot_general(
@@ -166,32 +195,37 @@
         ]
         sums.append(jnp.zeros((4, tokens), F32))
         out_ref[pl.ds(pl.multiple_of(owner * 8, 8), 8), :] = jnp.concatenate(sums, axis=0)
-
-
-def gate_dots(core, ids, other_ids, other, got, act, grad):
+    for copy in copies[2:]:
+        copy.wait()
+
+
+def gate_dots(core, ids, other_ids, other, got, other_rest, act, grad):
     tokens = act.shape[0]
     vmem, hbm = pl.BlockSpec(memory_space=pltpu.VMEM), pl.BlockSpec(memory_space=pltpu.HBM)
     return pl.pallas_call(
         dots_kernel,
-        in_specs=[pl.BlockSpec(memory_space=pltpu.SMEM)] + [vmem] * 4 + [hbm] * 2,
+        in_specs=[pl.BlockSpec(memory_space=pltpu.SMEM)] + [vmem] * 4 + [hbm] * 3,
         out_shape=(
             jax.ShapeDtypeStruct((16, tokens), F32),
             jax.ShapeDtypeStruct(other.shape, BF16),
+            jax.ShapeDtypeStruct(other.shape, BF16),
         ),
-        scratch_shapes=[pltpu.SemaphoreType.DMA((2,))],
+        scratch_shapes=[pltpu.SemaphoreType.DMA((4,))],
         compiler_params=BIG,
         name="gate_dots",
-    )(core, ids, other_ids, other, got, in_hbm(act), in_hbm(grad))
+    )(core, ids, other_ids, other, got, in_hbm(other_rest), in_hbm(act), in_hbm(grad))
 
 
 def score_kernel(
-    core_ref, mine_ref, theirs_ref, ids_ref, other_ids_ref, own_ref, other_ref, *outs
+    core_ref, mine_ref, theirs_ref, ids_ref, other_ids_ref, own_ref, other_ref, rest_ref, *outs
 ):
     score_grad_ref, part_ref = outs
-    rows, wide = part_ref.shape[0] // 2, part_ref.shape[1]
-    tokens, quarter = own_ref.shape[0] // 2, own_ref.shape[1] // 2
+    rows, quarter = part_ref.shape[0] // 2, part_ref.shape[1]
+    tokens = ids_ref.shape[1]
     core = core_ref[0]
     odd = odd_rows(rows, tokens)
+    row = iota((rows, tokens), 0)
+    expert = (row >> 3) * 8 + core * 4 + ((row >> 1) & 3)
     left = []
     for owner, ids in ((core, ids_ref[...]), (1 - core, other_ids_ref[...])):
         block = pl.ds(pl.multiple_of(owner * 8, 8), 8)
@@ -200,22 +234,20 @@
         score = [jax.nn.sigmoid(sums[2 + k : 3 + k, :]) for k in range(2)]
         total = score[0] + score[1]
         mean_term = (score[0] * gate[0] + score[1] * gate[1]) / total
-        named = named_rows(ids, rows)
         dense = jnp.zeros((rows, tokens), F32)
         for k in range(2):
             grad = route_scale / total * (gate[k] - mean_term) * score[k] * (1.0 - score[k])
             if not left:
                 score_grad_ref[k : k + 1, :] = grad
-            dense = jnp.where(named[k], grad, dense)
+            dense = jnp.where(expert == ids[k : k + 1, :], grad, dense)
         left += [jnp.where(odd, 0.0, dense).astype(BF16), jnp.where(odd, dense, 0.0).astype(BF16)]
     left = jnp.concatenate(left, axis=1)
-    rest = jnp.zeros((tokens, 2 * wide - quarter), BF16)
-    for side in range(2):
-        right = []
-        for halves_ref in (own_ref, other_ref):
-            act = halves_ref[:tokens, side * quarter : (side + 1) * quarter]
-            right += [act[:, :wide], jnp.concatenate([act[:, wide:], rest], axis=1)]
-        part_ref[side * rows : (side + 1) * rows, :] = jnp.dot(
+    for side, acts in (
+        (core, (own_ref[:tokens, :], other_ref[:tokens, :])),
+        (1 - core, (rest_ref[:tokens, :], rest_ref[tokens:, :])),
+    ):
+        right = [act[:, h * quarter : (h + 1) * quarter] for act in acts for h in range(2)]
+        part_ref[pl.ds(pl.multiple_of(side * rows, 16), rows), :] = jnp.dot(
             left, jnp.concatenate(right, axis=0), preferred_element_type=F32
         ).astype(BF16)
 
@@ -239,30 +271,19 @@
 
 def sum_kernel(got_ref, out_ref):
     rows, sources = out_ref.shape[0], got_ref.shape[0]
-    wide, columns = got_ref.shape[1], out_ref.shape[1]
-    row, col = iota((rows, sources), 0), iota((rows, sources), 1)
-    sent_by = (col & (sources // 2 - 1)) >= sources // 4
-    same = (row & 7) == jnp.where(sent_by, 4, 0) + ((col >> 1) & 3)
-    for h in range(2):
-        pick = ones_where(same & ((col & 1) == h))
-        start = h * wide
-        count = wide if h == 0 else columns - wide
-        out_ref[:, start : start + count] = jnp.dot(
-            pick, got_ref[:, :count], preferred_element_type=F32
-        ).astype(BF16)
+    pick = ones_where((iota((rows, sources), 0) & 7) == (iota((rows, sources), 1) & 7))
+    out_ref[...] = jnp.dot(pick, got_ref[...], preferred_element_type=F32).astype(BF16)
 
 
 def final_kernel(got_ref, out_ref):
     experts = out_ref.shape[0]
-    sources, quarter = got_ref.shape
+    sources, block = got_ref.shape
     row, col = iota((experts, sources), 0), iota((experts, sources), 1)
-    for half in range(2):
-        for side in range(2):
-            pick = ones_where((col & 15) == side * 8 + half * 4 + row)
-            start = (half * 2 + side) * quarter
-            out_ref[:, start : start + quarter] = jnp.dot(
-                pick, got_ref[...], preferred_element_type=F32
-            )
+    for piece in range(4):
+        pick = ones_where((col & 15) == ((piece >> 1) * 8 + row * 2 + (piece & 1)))
+        out_ref[:, piece * block : (piece + 1) * block] = jnp.dot(
+            pick, got_ref[...], preferred_element_type=F32
+        )
 
 
 def call(kernel, name, out_shape, *args, cost=None):
@@ -291,15 +312,17 @@
 
     packed = pack(saved_output.reshape(rows, width), router_weight)
     got = lax.all_to_all(packed, ("core", "chip"), split_axis=0, concat_axis=0, tiled=True)
-    other = swap(halves_for_other(core, activations, out_grad))
+    other, other_rest = [swap(x) for x in halves_for_other(core, activations, out_grad)]
     other_ids = swap(ids)
-    mine, own = gate_dots(core, ids, other_ids, other, got, activations, out_grad)
+    mine, own, rest = gate_dots(
+        core, ids, other_ids, other, got, other_rest, activations, out_grad
+    )
     score_grad, part = call(
         score_kernel,
         "scores",
         (
             jax.ShapeDtypeStruct((2, tokens), F32),
-            jax.ShapeDtypeStruct((2 * rows, WIDE), BF16),
+            jax.ShapeDtypeStruct((rows, width // 4), BF16),
         ),
         core,
         mine,
@@ -308,13 +331,12 @@
         other_ids,
         own,
         other,
-    )
-    part = lax.all_to_all(
-        part, ("side", "core", "chip"), split_axis=0, concat_axis=0, tiled=True
-    )
+        rest,
+    )
+    part = lax.all_to_all(part, ("side", "chip"), split_axis=0, concat_axis=0, tiled=True)
     summed = call(
         sum_kernel,
-        "sum_owners",
+        "sum_chips",
         jax.ShapeDtypeStruct((planes * 2 * experts, width // 4), BF16),
         part,
     )

time: 99.9 us -> 98 us (0.981)
  waiting for transfers between devices: 39.6 us -> 35.8 us
  starting transfers between devices: 31.3 us -> 33.4 us
  blocking collectives: 15.8 us -> 14.6 us
    all_to_all x1, waiting for transfers between devices: 23.9 us -> 20.7 us  [body(): lax.all_to_all(packed, ('core', 'chip'), split_axis=0, concat_axis=0, til...]
    ppermute x4 -> x5, starting transfers between devices: 8.21 us -> 10.3 us  [swap(): return lax.ppermute(x, 'core', [(0, 1), (1, 0)])]
    all_to_all x1, blocking collectives: 15.8 us -> 14.6 us  [body(): lax.all_to_all(part, ('side', 'chip'), split_axis=0, concat_axis=0, tiled...]
    ppermute x4 -> x5, waiting for transfers between devices: 3.71 us -> 3.82 us  [swap(): return lax.ppermute(x, 'core', [(0, 1), (1, 0)])]
  transfers between devices with their start and end apart: 6 -> 7, of which waited for: 5 -> 5; matrix products, arithmetic and copies ran while one was open for 0% -> 0% of each run, Pallas kernels for 3% -> 3%
where the time goes in v4:
time: 98 us; the launch traced here: 96.2 us
  waiting for transfers between devices  35.8 us (37%)
  starting transfers between devices  33.4 us (34%)
  blocking collectives  14.6 us (15%)
  Pallas kernels  10.8 us (11%)
    all_to_all x1, waiting for transfers between devices, body(): lax.all_to_all(packed, ('core', 'chip'), split_axis=0, concat_axis=0, til...  20.7 us
    all_to_all x1, blocking collectives, body(): lax.all_to_all(part, ('side', 'chip'), split_axis=0, concat_axis=0, tiled...  14.6 us
    all_to_all x1, starting transfers between devices, body(): lax.all_to_all(summed, ('pairs', 'side'), split_axis=0, concat_axis=0, ti...  13.5 us
    all_to_all x1, waiting for transfers between devices, body(): lax.all_to_all(summed, ('pairs', 'side'), split_axis=0, concat_axis=0, ti...  11.2 us
    ppermute x5, starting transfers between devices, swap(): return lax.ppermute(x, 'core', [(0, 1), (1, 0)])  10.3 us
    all_to_all x1, starting transfers between devices, body(): lax.all_to_all(packed, ('core', 'chip'), split_axis=0, concat_axis=0, til...  9.59 us
    pallas_call x4, Pallas kernels, call(): pl.pallas_call(kernel, in_specs=[pl.BlockSpec(memory_space=pltpu.SMEM if...  3.98 us
    ppermute x5, waiting for transfers between devices, swap(): return lax.ppermute(x, 'core', [(0, 1), (1, 0)])  3.82 us
  transfers between devices with their start and end apart: 7, of which 5 were waited for; matrix products, arithmetic and copies ran while one was open for 0% of the time, Pallas kernels for 3%

profile of v4, /device:TPU:6, one launch (start us, length us, event | category | flops | bytes accessed | tf_op | source)
XLA Modules:
  0.0 96.2 jit_solution(14004406873374506498)
XLA Ops:
  0.6 3.3 %pack_rows.1 = bf16[256,4480]{1,0:T(8,128)(2,1)} custom-call(bf16[256,3584]{1,0:T(8,128)(2,1)} %bitcast.21, bf16[4,3584]{1,0:T(4,128)(2,1)} %weight_hbm.1), custom_call_target="tpu_custom_call" | custom-call | tf_op jit(solution)/shard_map/pack_rows/pallas_call | solution.py:63
  3.9 0.0 copy-start
  3.9 9.6 %all-to-all-start = ((bf16[32,8,4480]{2,1,0:T(8,128)(2,1)}), bf16[32,8,4480]{2,1,0:T(8,128)(2,1)S(1)}, u32[]{:S(2)}, u32[]{:S(2)}) async-start(bf16[32,8,4480]{2,1,0:T(8,128)(2,1)} %bitcast.20), calls=%async_computation | async-start | bytes 4587520 | tf_op jit(solution)/shard_map/all_to_all | solution.py:314
  13.5 1.3 %halves_for_other.1 = (bf16[256,1792]{1,0:T(8,128)(2,1)S(1)}, bf16[128,1792]{1,0:T(8,128)(2,1)S(1)}) custom-call(s32[1]{0:T(128)} %bitcast.core_ref, bf16[128,3584]{1,0:T(8,128)(2,1)} %act_hbm.3, bf16[128,3584]{1,0:T(8,128)(2,1)} %grad_hbm.3), custom_call_target="tpu_custom_call" | custom-call | tf_op jit(solution)/shard_map/halves_for_other/pallas_call | solution.py:112
  14.9 2.1 %collective-permute-start.1 = (bf16[256,1792]{1,0:T(8,128)(2,1)S(1)}, bf16[256,1792]{1,0:T(8,128)(2,1)S(1)}, u32[]{:S(2)}, u32[]{:S(2)}) collective-permute-start(bf16[256,1792]{1,0:T(8,128)(2,1)S(1)} %get-tuple-element.12), channel_id=1, source_target_pairs={{0,1},{1,0},{2,3},{3,2},{4,5},{5,4},{6,7},{7,6},{8,9},{9,8},{10,11... | collective-permute-start | bytes 2752520 | tf_op jit(solution)/shard_map/ppermute | solution.py:311
  17.0 2.2 %collective-permute-start.2 = (bf16[128,1792]{1,0:T(8,128)(2,1)S(1)}, bf16[128,1792]{1,0:T(8,128)(2,1)S(1)}, u32[]{:S(2)}, u32[]{:S(2)}) collective-permute-start(bf16[128,1792]{1,0:T(8,128)(2,1)S(1)} %get-tuple-element.13), channel_id=1, source_target_pairs={{0,1},{1,0},{2,3},{3,2},{4,5},{5,4},{6,7},{7,6},{8,9},{9,8},{10,11... | collective-permute-start | bytes 1376264 | tf_op jit(solution)/shard_map/ppermute | solution.py:311
  19.2 0.0 copy-done
  19.2 2.1 %collective-permute-start = (s32[2,128]{1,0:T(2,128)S(1)}, s32[2,128]{1,0:T(2,128)S(1)}, u32[]{:S(2)}, u32[]{:S(2)}) collective-permute-start(s32[2,128]{1,0:T(2,128)S(1)} %bitcast.15), channel_id=1, source_target_pairs={{0,1},{1,0},{2,3},{3,2},{4,5},{5,4},{6,7},{7,6},{8,9},{9,8},{10,11... | collective-permute-start | bytes 3080 | tf_op jit(solution)/shard_map/ppermute | solution.py:311
  21.3 0.9 collective-permute-done.other_ids_ref
  22.2 0.0 collective-permute-done.2.other_rest_hbm
  22.2 0.0 copy-start.2
  22.2 0.8 copy-done.2
  23.0 0.0 collective-permute-done.1.other_ref
  23.0 20.7 %all-to-all-done = bf16[32,8,4480]{2,1,0:T(8,128)(2,1)S(1)} async-done(((bf16[32,8,4480]{2,1,0:T(8,128)(2,1)}), bf16[32,8,4480]{2,1,0:T(8,128)(2,1)S(1)}, u32[]{:S(2)}, u32[]{:S(2)}) %all-to-all-start) | async-done | bytes 2293792 | tf_op jit(solution)/shard_map/all_to_all | solution.py:314
  43.8 2.2 %gate_dots.1 = (f32[16,128]{1,0:T(8,128)S(1)}, bf16[256,1792]{1,0:T(8,128)(2,1)S(1)}, bf16[256,1792]{1,0:T(8,128)(2,1)S(1)}) custom-call(s32[1]{0:T(128)} %bitcast.core_ref, s32[2,128]{1,0:T(2,128)S(1)} %bitcast.16, s32[2,128]{1,0:T(2,128)S(1)} %collective-permute-done.other_ids_ref, bf16[256,1792]{1,0:T(8,128)(2,1)S(1)} %collective-permute-done.1.other_ref, ...), custom_call_target="tpu_custom_call" | custom-call | tf_op jit(solution)/shard_map/gate_dots/pallas_call | solution.py:205
  46.0 1.9 %collective-permute-start.3 = (f32[16,128]{1,0:T(8,128)S(1)}, f32[16,128]{1,0:T(8,128)S(1)}, u32[]{:S(2)}, u32[]{:S(2)}) collective-permute-start(f32[16,128]{1,0:T(8,128)S(1)} %get-tuple-element.14.mine_ref), channel_id=1, source_target_pairs={{0,1},{1,0},{2,3},{3,2},{4,5},{5,4},{6,7},{7,6},{8,9},{9,8},{10,11... | collective-permute-start | bytes 24584 | tf_op jit(solution)/shard_map/ppermute | solution.py:311
  47.9 1.1 %collective-permute-done.3.theirs_ref = f32[16,128]{1,0:T(8,128)S(1)} collective-permute-done((f32[16,128]{1,0:T(8,128)S(1)}, f32[16,128]{1,0:T(8,128)S(1)}, u32[]{:S(2)}, u32[]{:S(2)}) %collective-permute-start.3) | collective-permute-done | bytes 8224 | tf_op jit(solution)/shard_map/ppermute | solution.py:311
  49.1 0.7 scores.1
  49.8 0.0 copy-start.1
  49.8 14.6 %all_to_all.33 = bf16[32,8,896]{2,1,0:T(8,128)(2,1)S(1)} all-to-all(bf16[32,8,896]{2,1,0:T(8,128)(2,1)S(1)} %bitcast.14), channel_id=1, replica_groups=mesh['pairs'=8,'side'=2,'chip'=16,'core'=2] {'side','chip'}, dimensions={0} | all-to-all | bytes 917504 | tf_op jit(solution)/shard_map/all_to_all | solution.py:336
  64.4 0.9 sum_chips.1
  65.3 13.5 %all-to-all-start.2 = ((bf16[16,8,896]{2,1,0:T(8,128)(2,1)}), bf16[16,8,896]{2,1,0:T(8,128)(2,1)S(1)}, u32[]{:S(2)}, u32[]{:S(2)}) async-start(bf16[16,8,896]{2,1,0:T(8,128)(2,1)} %bitcast.8), calls=%async_computation.2 | async-start | bytes 458752 | tf_op jit(solution)/shard_map/all_to_all | solution.py:358
  78.9 1.9 %collective-permute-start.4 = (bf16[256,896]{1,0:T(8,128)(2,1)S(1)}, bf16[256,896]{1,0:T(8,128)(2,1)S(1)}, u32[]{:S(2)}, u32[]{:S(2)}) collective-permute-start(bf16[256,896]{1,0:T(8,128)(2,1)S(1)} %slice.3.own_ref), channel_id=1, source_target_pairs={{0,1},{1,0},{2,3},{3,2},{4,5},{5,4},{6,7},{7,6},{8,9},{9,8},{10,11... | collective-permute-start | bytes 1376264 | tf_op jit(solution)/shard_map/ppermute | solution.py:311
  80.8 1.8 %collective-permute-done.4.other_ref = bf16[256,896]{1,0:T(8,128)(2,1)S(1)} collective-permute-done((bf16[256,896]{1,0:T(8,128)(2,1)S(1)}, bf16[256,896]{1,0:T(8,128)(2,1)S(1)}, u32[]{:S(2)}, u32[]{:S(2)}) %collective-permute-start.4) | collective-permute-done | bytes 458784 | tf_op jit(solution)/shard_map/ppermute | solution.py:311
  82.6 0.0 copy-done.1
  82.6 1.4 %input_grads.1 = bf16[128,3584]{1,0:T(8,128)(2,1)} custom-call(s32[1]{0:T(128)} %bitcast.core_ref, s32[2,128]{1,0:T(2,128)S(1)} %bitcast.18, f32[2,128]{1,0:T(2,128)S(1)} %copy-done.1, bf16[256,896]{1,0:T(8,128)(2,1)S(1)} %slice.3.own_ref, bf16[256,896]{1,0:T(8,128)(2,1)S(1)} %collective-permute-done.4.other_ref), custom_call_target="tpu_custom_call" | custom-call | flops 234881024 | bytes 1835008 | tf_op jit(solution)/shard_map/input_grads/pallas_call | solution.py:290
  84.1 11.2 %all-to-all-done.2 = bf16[16,8,896]{2,1,0:T(8,128)(2,1)S(1)} async-done(((bf16[16,8,896]{2,1,0:T(8,128)(2,1)}), bf16[16,8,896]{2,1,0:T(8,128)(2,1)S(1)}, u32[]{:S(2)}, u32[]{:S(2)}) %all-to-all-start.2) | async-done | bytes 229408 | tf_op jit(solution)/shard_map/all_to_all | solution.py:358
  95.3 0.9 sum_batches.1
  (1 shorter events, 0.0 us)
Async XLA Ops:
  3.9 15.3 %copy-start = (s32[128,2]{0,1:T(2,128)S(1)}, s32[128,2]{0,1:T(2,128)}, u32[]{:S(2)}) copy-start(s32[128,2]{0,1:T(2,128)} %param.8) | copy-start | bytes 3076
  3.9 39.8 %all-to-all-start = ((bf16[32,8,4480]{2,1,0:T(8,128)(2,1)}), bf16[32,8,4480]{2,1,0:T(8,128)(2,1)S(1)}, u32[]{:S(2)}, u32[]{:S(2)}) async-start(bf16[32,8,4480]{2,1,0:T(8,128)(2,1)} %bitcast.20), calls=%async_computation | async-start | bytes 4587520 | tf_op jit(solution)/shard_map/all_to_all | solution.py:314
  14.9 8.2 %collective-permute-start.1 = (bf16[256,1792]{1,0:T(8,128)(2,1)S(1)}, bf16[256,1792]{1,0:T(8,128)(2,1)S(1)}, u32[]{:S(2)}, u32[]{:S(2)}) collective-permute-start(bf16[256,1792]{1,0:T(8,128)(2,1)S(1)} %get-tuple-element.12), channel_id=1, source_target_pairs={{0,1},{1,0},{2,3},{3,2},{4,5},{5,4},{6,7},{7,6},{8,9},{9,8},{10,11... | collective-permute-start | bytes 2752520 | tf_op jit(solution)/shard_map/ppermute | solution.py:311
  17.0 5.2 %collective-permute-start.2 = (bf16[128,1792]{1,0:T(8,128)(2,1)S(1)}, bf16[128,1792]{1,0:T(8,128)(2,1)S(1)}, u32[]{:S(2)}, u32[]{:S(2)}) collective-permute-start(bf16[128,1792]{1,0:T(8,128)(2,1)S(1)} %get-tuple-element.13), channel_id=1, source_target_pairs={{0,1},{1,0},{2,3},{3,2},{4,5},{5,4},{6,7},{7,6},{8,9},{9,8},{10,11... | collective-permute-start | bytes 1376264 | tf_op jit(solution)/shard_map/ppermute | solution.py:311
  19.2 3.0 %collective-permute-start = (s32[2,128]{1,0:T(2,128)S(1)}, s32[2,128]{1,0:T(2,128)S(1)}, u32[]{:S(2)}, u32[]{:S(2)}) collective-permute-start(s32[2,128]{1,0:T(2,128)S(1)} %bitcast.15), channel_id=1, source_target_pairs={{0,1},{1,0},{2,3},{3,2},{4,5},{5,4},{6,7},{7,6},{8,9},{9,8},{10,11... | collective-permute-start | bytes 3080 | tf_op jit(solution)/shard_map/ppermute | solution.py:311
  22.2 0.8 copy-start.2
  46.0 3.1 %collective-permute-start.3 = (f32[16,128]{1,0:T(8,128)S(1)}, f32[16,128]{1,0:T(8,128)S(1)}, u32[]{:S(2)}, u32[]{:S(2)}) collective-permute-start(f32[16,128]{1,0:T(8,128)S(1)} %get-tuple-element.14.mine_ref), channel_id=1, source_target_pairs={{0,1},{1,0},{2,3},{3,2},{4,5},{5,4},{6,7},{7,6},{8,9},{9,8},{10,11... | collective-permute-start | bytes 24584 | tf_op jit(solution)/shard_map/ppermute | solution.py:311
  49.8 32.8 %copy-start.1 = (f32[2,128]{1,0:T(2,128)S(1)}, f32[2,128]{1,0:T(2,128)}, u32[]{:S(2)}) copy-start(f32[2,128]{1,0:T(2,128)} %get-tuple-element.17.score_grad_ref) | copy-start | bytes 3076
  65.3 30.0 %all-to-all-start.2 = ((bf16[16,8,896]{2,1,0:T(8,128)(2,1)}), bf16[16,8,896]{2,1,0:T(8,128)(2,1)S(1)}, u32[]{:S(2)}, u32[]{:S(2)}) async-start(bf16[16,8,896]{2,1,0:T(8,128)(2,1)} %bitcast.8), calls=%async_computation.2 | async-start | bytes 458752 | tf_op jit(solution)/shard_map/all_to_all | solution.py:358
  78.9 3.7 %collective-permute-start.4 = (bf16[256,896]{1,0:T(8,128)(2,1)S(1)}, bf16[256,896]{1,0:T(8,128)(2,1)S(1)}, u32[]{:S(2)}, u32[]{:S(2)}) collective-permute-start(bf16[256,896]{1,0:T(8,128)(2,1)S(1)} %slice.3.own_ref), channel_id=1, source_target_pairs={{0,1},{1,0},{2,3},{3,2},{4,5},{5,4},{6,7},{7,6},{8,9},{9,8},{10,11... | collective-permute-start | bytes 1376264 | tf_op jit(solution)/shard_map/ppermute | solution.py:311

commit v5 on v4

--- a/solution.py
+++ b/solution.py
@@ -9,11 +9,16 @@
 BF16, F32 = jnp.bfloat16, jnp.float32
 NT = (((1,), (1,)), ((), ()))
 TN = (((0,), (0,)), ((), ()))
+CHIP, PLANE = 10, 10
 BIG = pltpu.CompilerParams(vmem_limit_bytes=40 * 1024 * 1024)
 
 
 def iota(shape, dim):
     return lax.broadcasted_iota(jnp.int32, shape, dim)
+
+
+def chip_at(place, chips):
+    return (place + CHIP) & (chips - 1)
 
 
 def ones_where(mask):
@@ -33,14 +38,15 @@
         copies[i].start()
     row, col = iota((rows, rows), 0), iota((rows, rows), 1)
     local = row & (per_core - 1)
-    source = ((local >> 1) & 3) * (rows // 4) + (local >> 3) * 4 + (local & 1)
+    chip = chip_at(local >> 3, per_core // 8)
+    source = ((local >> 1) & 3) * (rows // 4) + chip * 4 + (local & 1)
     pick = ones_where(col == source + jnp.where(row < per_core, 0, 2))
     row, col = iota((per_core, 8), 0), iota((per_core, 8), 1)
     pick_weight = ones_where(col == ((row >> 1) & 3) + (row & 1) * 4)
     copies[2].wait()
     sent = []
     for k, block in enumerate(halves):
-        mine = slice(k * per_core, (k + 1) * per_core)
+        mine = slice((1 - k) * per_core, (2 - k) * per_core)
         parts = [
             weight_ref[:, k * half + m * quarter : k * half + (m + 1) * quarter] for m in range(2)
         ]
@@ -125,8 +131,8 @@
 
 def named_rows(ids, rows):
     row = iota((rows, ids.shape[1]), 0)
-    chips = rows // 16
-    expert = ((row >> 3) & (chips - 1)) * 8 + (row >= rows // 2) * 4 + ((row >> 1) & 3)
+    chip = chip_at(row >> 3, rows // 16)
+    expert = chip * 8 + (row < rows // 2) * 4 + ((row >> 1) & 3)
     return [expert == ids[k : k + 1, :] for k in range(2)]
 
 
@@ -225,7 +231,7 @@
     core = core_ref[0]
     odd = odd_rows(rows, tokens)
     row = iota((rows, tokens), 0)
-    expert = (row >> 3) * 8 + core * 4 + ((row >> 1) & 3)
+    expert = chip_at(row >> 3, rows // 8) * 8 + core * 4 + ((row >> 1) & 3)
     left = []
     for owner, ids in ((core, ids_ref[...]), (1 - core, other_ids_ref[...])):
         block = pl.ds(pl.multiple_of(owner * 8, 8), 8)
@@ -299,10 +305,18 @@
     )(*args)
 
 
+def exchange(x, axes, order):
+    return lax.all_to_all(
+        x, axes, split_axis=0, concat_axis=0, tiled=True, axis_index_groups=[order]
+    )
+
+
 def body(activations, out_grad, router_weight, expert_ids, saved_output):
     experts, width = router_weight.shape
     tokens = activations.shape[0]
     planes = lax.axis_size("pairs") * lax.axis_size("side")
+    chips = lax.axis_size("chip")
+    chip_order = [chip_at(i, chips) for i in range(chips)]
     rows = experts * saved_output.shape[2]
     core = lax.axis_index("core").astype(jnp.int32).reshape(1)
     ids = expert_ids.T
@@ -311,7 +325,8 @@
         return lax.ppermute(x, "core", [(0, 1), (1, 0)])
 
     packed = pack(saved_output.reshape(rows, width), router_weight)
-    got = lax.all_to_all(packed, ("core", "chip"), split_axis=0, concat_axis=0, tiled=True)
+    order = [core * chips + chip for core in (1, 0) for chip in chip_order]
+    got = exchange(packed, ("core", "chip"), order)
     other, other_rest = [swap(x) for x in halves_for_other(core, activations, out_grad)]
     other_ids = swap(ids)
     mine, own, rest = gate_dots(
@@ -333,7 +348,8 @@
         other,
         rest,
     )
-    part = lax.all_to_all(part, ("side", "chip"), split_axis=0, concat_axis=0, tiled=True)
+    order = [side * chips + chip for side in (0, 1) for chip in chip_order]
+    part = exchange(part, ("side", "chip"), order)
     summed = call(
         sum_kernel,
         "sum_chips",
@@ -355,7 +371,7 @@
             flops=2 * tokens * rows * width, bytes_accessed=4 * tokens * width, transcendentals=0
         ),
     )
-    summed = lax.all_to_all(summed, ("pairs", "side"), split_axis=0, concat_axis=0, tiled=True)
+    summed = exchange(summed, ("pairs", "side"), [(i + PLANE) % planes for i in range(planes)])
     router_grad = call(
         final_kernel, "sum_batches", jax.ShapeDtypeStruct((experts, width), F32), summed
     )

time: 98 us -> 91.4 us (0.933); the launches traced: 96.2 us -> 90.9 us
  waiting for transfers between devices: 35.8 us -> 30 us
    all_to_all x2, waiting for transfers between devices: 32 us -> 26 us  [exchange(): lax.all_to_all(x, axes, split_axis=0, concat_axis=0, tiled=True, axis_ind...]
where the time goes in v5:
time: 91.4 us; the launch traced here: 90.9 us
  starting transfers between devices  33.7 us (37%)
  waiting for transfers between devices  30 us (33%)
  blocking collectives  14.8 us (16%)
  Pallas kernels  10.8 us (12%)
    all_to_all x2, waiting for transfers between devices, exchange(): lax.all_to_all(x, axes, split_axis=0, concat_axis=0, tiled=True, axis_ind...  26 us
    all_to_all x2, starting transfers between devices, exchange(): lax.all_to_all(x, axes, split_axis=0, concat_axis=0, tiled=True, axis_ind...  23.6 us
    all_to_all x1, blocking collectives, exchange(): lax.all_to_all(x, axes, split_axis=0, concat_axis=0, tiled=True, axis_ind...  14.8 us
    ppermute x5, starting transfers between devices, swap(): return lax.ppermute(x, 'core', [(0, 1), (1, 0)])  10.1 us
    pallas_call x4, Pallas kernels, call(): pl.pallas_call(kernel, in_specs=[pl.BlockSpec(memory_space=pltpu.SMEM if...  4 us
    ppermute x5, waiting for transfers between devices, swap(): return lax.ppermute(x, 'core', [(0, 1), (1, 0)])  3.97 us
    pallas_call x1, Pallas kernels, pack(): pl.pallas_call(pack_kernel, in_specs=[pl.BlockSpec(memory_space=pltpu.HBM...  3.29 us
    pallas_call x1, Pallas kernels, gate_dots(): pl.pallas_call(dots_kernel, in_specs=[pl.BlockSpec(memory_space=pltpu.SME...  2.23 us
  transfers between devices with their start and end apart: 7, of which 5 were waited for; matrix products, arithmetic and copies ran while one was open for 0% of the time, Pallas kernels for 3%

profile of v5, /device:TPU:6, one launch (start us, length us, event | category | flops | bytes accessed | tf_op | source)
XLA Modules:
  0.0 90.9 jit_solution(15583374412461006336)
XLA Ops:
  0.6 3.3 %pack_rows.1 = bf16[256,4480]{1,0:T(8,128)(2,1)} custom-call(bf16[256,3584]{1,0:T(8,128)(2,1)} %bitcast.21, bf16[4,3584]{1,0:T(4,128)(2,1)} %weight_hbm.1), custom_call_target="tpu_custom_call" | custom-call | tf_op jit(solution)/shard_map/pack_rows/pallas_call | solution.py:69
  3.9 0.0 copy-start
  3.9 10.3 %all-to-all-start = ((bf16[32,8,4480]{2,1,0:T(8,128)(2,1)}), bf16[32,8,4480]{2,1,0:T(8,128)(2,1)S(1)}, u32[]{:S(2)}, u32[]{:S(2)}) async-start(bf16[32,8,4480]{2,1,0:T(8,128)(2,1)} %bitcast.20), calls=%async_computation | async-start | bytes 4587520 | tf_op jit(solution)/shard_map/all_to_all | solution.py:309
  14.3 1.3 %halves_for_other.1 = (bf16[256,1792]{1,0:T(8,128)(2,1)S(1)}, bf16[128,1792]{1,0:T(8,128)(2,1)S(1)}) custom-call(s32[1]{0:T(128)} %bitcast.core_ref, bf16[128,3584]{1,0:T(8,128)(2,1)} %act_hbm.3, bf16[128,3584]{1,0:T(8,128)(2,1)} %grad_hbm.3), custom_call_target="tpu_custom_call" | custom-call | tf_op jit(solution)/shard_map/halves_for_other/pallas_call | solution.py:118
  15.6 2.0 %collective-permute-start.1 = (bf16[256,1792]{1,0:T(8,128)(2,1)S(1)}, bf16[256,1792]{1,0:T(8,128)(2,1)S(1)}, u32[]{:S(2)}, u32[]{:S(2)}) collective-permute-start(bf16[256,1792]{1,0:T(8,128)(2,1)S(1)} %get-tuple-element.12), channel_id=1, source_target_pairs={{0,1},{1,0},{2,3},{3,2},{4,5},{5,4},{6,7},{7,6},{8,9},{9,8},{10,11... | collective-permute-start | bytes 2752520 | tf_op jit(solution)/shard_map/ppermute | solution.py:325
  17.6 2.4 %collective-permute-start.2 = (bf16[128,1792]{1,0:T(8,128)(2,1)S(1)}, bf16[128,1792]{1,0:T(8,128)(2,1)S(1)}, u32[]{:S(2)}, u32[]{:S(2)}) collective-permute-start(bf16[128,1792]{1,0:T(8,128)(2,1)S(1)} %get-tuple-element.13), channel_id=1, source_target_pairs={{0,1},{1,0},{2,3},{3,2},{4,5},{5,4},{6,7},{7,6},{8,9},{9,8},{10,11... | collective-permute-start | bytes 1376264 | tf_op jit(solution)/shard_map/ppermute | solution.py:325
  20.0 0.0 copy-done
  20.0 2.0 %collective-permute-start = (s32[2,128]{1,0:T(2,128)S(1)}, s32[2,128]{1,0:T(2,128)S(1)}, u32[]{:S(2)}, u32[]{:S(2)}) collective-permute-start(s32[2,128]{1,0:T(2,128)S(1)} %bitcast.15), channel_id=1, source_target_pairs={{0,1},{1,0},{2,3},{3,2},{4,5},{5,4},{6,7},{7,6},{8,9},{9,8},{10,11... | collective-permute-start | bytes 3080 | tf_op jit(solution)/shard_map/ppermute | solution.py:325
  21.9 1.0 %collective-permute-done.other_ids_ref = s32[2,128]{1,0:T(2,128)S(1)} collective-permute-done((s32[2,128]{1,0:T(2,128)S(1)}, s32[2,128]{1,0:T(2,128)S(1)}, u32[]{:S(2)}, u32[]{:S(2)}) %collective-permute-start) | collective-permute-done | bytes 1056 | tf_op jit(solution)/shard_map/ppermute | solution.py:325
  23.0 0.0 collective-permute-done.2.other_rest_hbm
  23.0 0.0 copy-start.2
  23.0 0.8 copy-done.2
  23.8 0.0 collective-permute-done.1.other_ref
  23.8 18.8 %all-to-all-done = bf16[32,8,4480]{2,1,0:T(8,128)(2,1)S(1)} async-done(((bf16[32,8,4480]{2,1,0:T(8,128)(2,1)}), bf16[32,8,4480]{2,1,0:T(8,128)(2,1)S(1)}, u32[]{:S(2)}, u32[]{:S(2)}) %all-to-all-start) | async-done | bytes 2293792 | tf_op jit(solution)/shard_map/all_to_all | solution.py:309
  42.6 2.2 %gate_dots.1 = (f32[16,128]{1,0:T(8,128)S(1)}, bf16[256,1792]{1,0:T(8,128)(2,1)S(1)}, bf16[256,1792]{1,0:T(8,128)(2,1)S(1)}) custom-call(s32[1]{0:T(128)} %bitcast.core_ref, s32[2,128]{1,0:T(2,128)S(1)} %bitcast.16, s32[2,128]{1,0:T(2,128)S(1)} %collective-permute-done.other_ids_ref, bf16[256,1792]{1,0:T(8,128)(2,1)S(1)} %collective-permute-done.1.other_ref, ...), custom_call_target="tpu_custom_call" | custom-call | tf_op jit(solution)/shard_map/gate_dots/pallas_call | solution.py:211
  44.8 1.9 %collective-permute-start.3 = (f32[16,128]{1,0:T(8,128)S(1)}, f32[16,128]{1,0:T(8,128)S(1)}, u32[]{:S(2)}, u32[]{:S(2)}) collective-permute-start(f32[16,128]{1,0:T(8,128)S(1)} %get-tuple-element.14.mine_ref), channel_id=1, source_target_pairs={{0,1},{1,0},{2,3},{3,2},{4,5},{5,4},{6,7},{7,6},{8,9},{9,8},{10,11... | collective-permute-start | bytes 24584 | tf_op jit(solution)/shard_map/ppermute | solution.py:325
  46.7 1.1 %collective-permute-done.3.theirs_ref = f32[16,128]{1,0:T(8,128)S(1)} collective-permute-done((f32[16,128]{1,0:T(8,128)S(1)}, f32[16,128]{1,0:T(8,128)S(1)}, u32[]{:S(2)}, u32[]{:S(2)}) %collective-permute-start.3) | collective-permute-done | bytes 8224 | tf_op jit(solution)/shard_map/ppermute | solution.py:325
  47.9 0.7 scores.1
  48.6 0.0 copy-start.1
  48.6 14.8 %all_to_all.33 = bf16[32,8,896]{2,1,0:T(8,128)(2,1)S(1)} all-to-all(bf16[32,8,896]{2,1,0:T(8,128)(2,1)S(1)} %bitcast.14), channel_id=1, replica_groups={{20,22,24,26,28,30,0,2,4,6,8,10,12,14,16,18,52,54,56,58,60,62,32,34,36,..., dimensions={0} | all-to-all | bytes 917504 | tf_op jit(solution)/shard_map/all_to_all | solution.py:309
  63.5 0.9 %sum_chips.1 = bf16[128,896]{1,0:T(8,128)(2,1)} custom-call(bf16[256,896]{1,0:T(8,128)(2,1)S(1)} %bitcast.12), custom_call_target="tpu_custom_call" | custom-call | tf_op jit(solution)/shard_map/sum_chips/pallas_call | solution.py:296
  64.4 13.2 %all-to-all-start.2 = ((bf16[16,8,896]{2,1,0:T(8,128)(2,1)}), bf16[16,8,896]{2,1,0:T(8,128)(2,1)S(1)}, u32[]{:S(2)}, u32[]{:S(2)}) async-start(bf16[16,8,896]{2,1,0:T(8,128)(2,1)} %bitcast.8), calls=%async_computation.2 | async-start | bytes 458752 | tf_op jit(solution)/shard_map/all_to_all | solution.py:309
  77.6 1.9 %collective-permute-start.4 = (bf16[256,896]{1,0:T(8,128)(2,1)S(1)}, bf16[256,896]{1,0:T(8,128)(2,1)S(1)}, u32[]{:S(2)}, u32[]{:S(2)}) collective-permute-start(bf16[256,896]{1,0:T(8,128)(2,1)S(1)} %slice.3.own_ref), channel_id=1, source_target_pairs={{0,1},{1,0},{2,3},{3,2},{4,5},{5,4},{6,7},{7,6},{8,9},{9,8},{10,11... | collective-permute-start | bytes 1376264 | tf_op jit(solution)/shard_map/ppermute | solution.py:325
  79.6 1.8 %collective-permute-done.4.other_ref = bf16[256,896]{1,0:T(8,128)(2,1)S(1)} collective-permute-done((bf16[256,896]{1,0:T(8,128)(2,1)S(1)}, bf16[256,896]{1,0:T(8,128)(2,1)S(1)}, u32[]{:S(2)}, u32[]{:S(2)}) %collective-permute-start.4) | collective-permute-done | bytes 458784 | tf_op jit(solution)/shard_map/ppermute | solution.py:325
  81.4 0.0 copy-done.1
  81.4 1.5 %input_grads.1 = bf16[128,3584]{1,0:T(8,128)(2,1)} custom-call(s32[1]{0:T(128)} %bitcast.core_ref, s32[2,128]{1,0:T(2,128)S(1)} %bitcast.18, f32[2,128]{1,0:T(2,128)S(1)} %copy-done.1, bf16[256,896]{1,0:T(8,128)(2,1)S(1)} %slice.3.own_ref, bf16[256,896]{1,0:T(8,128)(2,1)S(1)} %collective-permute-done.4.other_ref), custom_call_target="tpu_custom_call" | custom-call | flops 234881024 | bytes 1835008 | tf_op jit(solution)/shard_map/input_grads/pallas_call | solution.py:296
  82.8 7.2 %all-to-all-done.2 = bf16[16,8,896]{2,1,0:T(8,128)(2,1)S(1)} async-done(((bf16[16,8,896]{2,1,0:T(8,128)(2,1)}), bf16[16,8,896]{2,1,0:T(8,128)(2,1)S(1)}, u32[]{:S(2)}, u32[]{:S(2)}) %all-to-all-start.2) | async-done | bytes 229408 | tf_op jit(solution)/shard_map/all_to_all | solution.py:309
  90.0 0.9 sum_batches.1
  (1 shorter events, 0.0 us)
Async XLA Ops:
  3.9 16.0 %copy-start = (s32[128,2]{0,1:T(2,128)S(1)}, s32[128,2]{0,1:T(2,128)}, u32[]{:S(2)}) copy-start(s32[128,2]{0,1:T(2,128)} %param.8) | copy-start | bytes 3076
  3.9 38.6 %all-to-all-start = ((bf16[32,8,4480]{2,1,0:T(8,128)(2,1)}), bf16[32,8,4480]{2,1,0:T(8,128)(2,1)S(1)}, u32[]{:S(2)}, u32[]{:S(2)}) async-start(bf16[32,8,4480]{2,1,0:T(8,128)(2,1)} %bitcast.20), calls=%async_computation | async-start | bytes 4587520 | tf_op jit(solution)/shard_map/all_to_all | solution.py:309
  15.6 8.2 %collective-permute-start.1 = (bf16[256,1792]{1,0:T(8,128)(2,1)S(1)}, bf16[256,1792]{1,0:T(8,128)(2,1)S(1)}, u32[]{:S(2)}, u32[]{:S(2)}) collective-permute-start(bf16[256,1792]{1,0:T(8,128)(2,1)S(1)} %get-tuple-element.12), channel_id=1, source_target_pairs={{0,1},{1,0},{2,3},{3,2},{4,5},{5,4},{6,7},{7,6},{8,9},{9,8},{10,11... | collective-permute-start | bytes 2752520 | tf_op jit(solution)/shard_map/ppermute | solution.py:325
  17.6 5.4 %collective-permute-start.2 = (bf16[128,1792]{1,0:T(8,128)(2,1)S(1)}, bf16[128,1792]{1,0:T(8,128)(2,1)S(1)}, u32[]{:S(2)}, u32[]{:S(2)}) collective-permute-start(bf16[128,1792]{1,0:T(8,128)(2,1)S(1)} %get-tuple-element.13), channel_id=1, source_target_pairs={{0,1},{1,0},{2,3},{3,2},{4,5},{5,4},{6,7},{7,6},{8,9},{9,8},{10,11... | collective-permute-start | bytes 1376264 | tf_op jit(solution)/shard_map/ppermute | solution.py:325
  20.0 3.0 %collective-permute-start = (s32[2,128]{1,0:T(2,128)S(1)}, s32[2,128]{1,0:T(2,128)S(1)}, u32[]{:S(2)}, u32[]{:S(2)}) collective-permute-start(s32[2,128]{1,0:T(2,128)S(1)} %bitcast.15), channel_id=1, source_target_pairs={{0,1},{1,0},{2,3},{3,2},{4,5},{5,4},{6,7},{7,6},{8,9},{9,8},{10,11... | collective-permute-start | bytes 3080 | tf_op jit(solution)/shard_map/ppermute | solution.py:325
  23.0 0.8 copy-start.2
  44.8 3.1 %collective-permute-start.3 = (f32[16,128]{1,0:T(8,128)S(1)}, f32[16,128]{1,0:T(8,128)S(1)}, u32[]{:S(2)}, u32[]{:S(2)}) collective-permute-start(f32[16,128]{1,0:T(8,128)S(1)} %get-tuple-element.14.mine_ref), channel_id=1, source_target_pairs={{0,1},{1,0},{2,3},{3,2},{4,5},{5,4},{6,7},{7,6},{8,9},{9,8},{10,11... | collective-permute-start | bytes 24584 | tf_op jit(solution)/shard_map/ppermute | solution.py:325
  48.6 32.7 %copy-start.1 = (f32[2,128]{1,0:T(2,128)S(1)}, f32[2,128]{1,0:T(2,128)}, u32[]{:S(2)}) copy-start(f32[2,128]{1,0:T(2,128)} %get-tuple-element.17.score_grad_ref) | copy-start | bytes 3076
  64.4 25.6 %all-to-all-start.2 = ((bf16[16,8,896]{2,1,0:T(8,128)(2,1)}), bf16[16,8,896]{2,1,0:T(8,128)(2,1)S(1)}, u32[]{:S(2)}, u32[]{:S(2)}) async-start(bf16[16,8,896]{2,1,0:T(8,128)(2,1)} %bitcast.8), calls=%async_computation.2 | async-start | bytes 458752 | tf_op jit(solution)/shard_map/all_to_all | solution.py:309
  77.6 3.7 %collective-permute-start.4 = (bf16[256,896]{1,0:T(8,128)(2,1)S(1)}, bf16[256,896]{1,0:T(8,128)(2,1)S(1)}, u32[]{:S(2)}, u32[]{:S(2)}) collective-permute-start(bf16[256,896]{1,0:T(8,128)(2,1)S(1)} %slice.3.own_ref), channel_id=1, source_target_pairs={{0,1},{1,0},{2,3},{3,2},{4,5},{5,4},{6,7},{7,6},{8,9},{9,8},{10,11... | collective-permute-start | bytes 1376264 | tf_op jit(solution)/shard_map/ppermute | solution.py:325

commit v6 on v5

--- a/solution.py
+++ b/solution.py
@@ -54,11 +54,19 @@
             pick_weight, jnp.concatenate(parts, axis=0), preferred_element_type=F32
         ).astype(BF16)
         copies[k].wait()
-        out = jnp.dot(pick, saved_ref[:, block], preferred_element_type=F32).astype(BF16)
         for core in range(2):
-            out_ref[mine, halves[core]] = out[core * per_core : (core + 1) * per_core]
-        sent.append(pltpu.make_async_copy(out_ref.at[mine], out_hbm.at[mine], out_sem.at[k]))
-        sent[k].start()
+            out_ref[mine, halves[core]] = jnp.dot(
+                pick[core * per_core : (core + 1) * per_core],
+                saved_ref[:, block],
+                preferred_element_type=F32,
+            ).astype(BF16)
+            columns = slice(0, half) if core == 0 else slice(half, width + quarter)
+            sent.append(
+                pltpu.make_async_copy(
+                    out_ref.at[mine, columns], out_hbm.at[mine, columns], out_sem.at[len(sent)]
+                )
+            )
+            sent[-1].start()
     for copy in sent:
         copy.wait()
 
@@ -76,7 +84,7 @@
             pltpu.VMEM(weight.shape, BF16),
             pltpu.VMEM(packed, BF16),
             pltpu.SemaphoreType.DMA((3,)),
-            pltpu.SemaphoreType.DMA((2,)),
+            pltpu.SemaphoreType.DMA((4,)),
         ],
         compiler_params=BIG,
         name="pack_rows",
@@ -96,7 +104,7 @@
     return copies
 
 
-def halves_kernel(core_ref, act_hbm, grad_hbm, out_ref, rest_ref, sem):
+def halves_kernel(core_ref, act_hbm, grad_hbm, out_ref, rest_ref, own_rest_ref, sem):
     tokens = act_hbm.shape[0]
     mine, theirs = core_ref[0], 1 - core_ref[0]
     copies = half_copies(
@@ -104,6 +112,7 @@
             (act_hbm, theirs, out_ref.at[pl.ds(0, tokens)]),
             (grad_hbm, theirs, out_ref.at[pl.ds(tokens, tokens)]),
             (act_hbm, mine, rest_ref),
+            (act_hbm, theirs, own_rest_ref),
         ],
         sem,
     )
@@ -122,8 +131,9 @@
         out_shape=(
             jax.ShapeDtypeStruct((2 * tokens, width // 2), BF16),
             jax.ShapeDtypeStruct((tokens, width // 2), BF16),
+            pltpu.HBM((tokens, width // 2), BF16),
         ),
-        scratch_shapes=[pltpu.SemaphoreType.DMA((3,))],
+        scratch_shapes=[pltpu.SemaphoreType.DMA((4,))],
         compiler_params=BIG,
         name="halves_for_other",
     )(core, in_hbm(act), in_hbm(grad))
@@ -146,12 +156,10 @@
     other_ids_ref,
     other_ref,
     got_ref,
-    other_rest_hbm,
     act_hbm,
     grad_hbm,
     out_ref,
     own_ref,
-    rest_ref,
     sem,
 ):
     rows = got_ref.shape[0]
@@ -163,8 +171,6 @@
         [
             (act_hbm, core, own_ref.at[low]),
             (grad_hbm, core, own_ref.at[high]),
-            (act_hbm, 1 - core, rest_ref.at[low]),
-            (other_rest_hbm, 0, rest_ref.at[high]),
         ],
         sem,
     )
@@ -177,7 +183,7 @@
         (core, ids_ref[...], own_ref),
     ):
         if halves_ref is own_ref:
-            for copy in copies[:2]:
+            for copy in copies:
                 copy.wait()
         saved = got_ref[:, pl.ds(pl.multiple_of(owner * half, 128), half)]
         dots = lax.dot_general(
@@ -201,25 +207,45 @@
         ]
         sums.append(jnp.zeros((4, tokens), F32))
         out_ref[pl.ds(pl.multiple_of(owner * 8, 8), 8), :] = jnp.concatenate(sums, axis=0)
-    for copy in copies[2:]:
+
+
+def stage_kernel(own_hbm, other_hbm, out_ref, sem):
+    tokens = own_hbm.shape[0]
+    copies = [
+        pltpu.make_async_copy(array, out_ref.at[pl.ds(i * tokens, tokens)], sem.at[i])
+        for i, array in enumerate((own_hbm, other_hbm))
+    ]
+    for copy in copies:
+        copy.start()
+    for copy in copies:
         copy.wait()
 
 
-def gate_dots(core, ids, other_ids, other, got, other_rest, act, grad):
+def stage(own, other):
+    return pl.pallas_call(
+        stage_kernel,
+        in_specs=[pl.BlockSpec(memory_space=pltpu.HBM)] * 2,
+        out_shape=jax.ShapeDtypeStruct((2 * own.shape[0], own.shape[1]), BF16),
+        scratch_shapes=[pltpu.SemaphoreType.DMA((2,))],
+        compiler_params=BIG,
+        name="stage",
+    )(in_hbm(own), in_hbm(other))
+
+
+def gate_dots(core, ids, other_ids, other, got, act, grad):
     tokens = act.shape[0]
     vmem, hbm = pl.BlockSpec(memory_space=pltpu.VMEM), pl.BlockSpec(memory_space=pltpu.HBM)
     return pl.pallas_call(
         dots_kernel,
-        in_specs=[pl.BlockSpec(memory_space=pltpu.SMEM)] + [vmem] * 4 + [hbm] * 3,
+        in_specs=[pl.BlockSpec(memory_space=pltpu.SMEM)] + [vmem] * 4 + [hbm] * 2,
         out_shape=(
             jax.ShapeDtypeStruct((16, tokens), F32),
             jax.ShapeDtypeStruct(other.shape, BF16),
-            jax.ShapeDtypeStruct(other.shape, BF16),
         ),
-        scratch_shapes=[pltpu.SemaphoreType.DMA((4,))],
+        scratch_shapes=[pltpu.SemaphoreType.DMA((2,))],
         compiler_params=BIG,
         name="gate_dots",
-    )(core, ids, other_ids, other, got, in_hbm(other_rest), in_hbm(act), in_hbm(grad))
+    )(core, ids, other_ids, other, got, in_hbm(act), in_hbm(grad))
 
 
 def score_kernel(
@@ -253,7 +279,7 @@
         (1 - core, (rest_ref[:tokens, :], rest_ref[tokens:, :])),
     ):
         right = [act[:, h * quarter : (h + 1) * quarter] for act in acts for h in range(2)]
-        part_ref[pl.ds(pl.multiple_of(side * rows, 16), rows), :] = jnp.dot(
+        part_ref[pl.ds(pl.multiple_of((1 - side) * rows, 16), rows), :] = jnp.dot(
             left, jnp.concatenate(right, axis=0), preferred_element_type=F32
         ).astype(BF16)
 
@@ -327,11 +353,13 @@
     packed = pack(saved_output.reshape(rows, width), router_weight)
     order = [core * chips + chip for core in (1, 0) for chip in chip_order]
     got = exchange(packed, ("core", "chip"), order)
-    other, other_rest = [swap(x) for x in halves_for_other(core, activations, out_grad)]
+    other, other_rest, own_rest = halves_for_other(core, activations, out_grad)
+    other, other_rest = swap(other), swap(other_rest)
     other_ids = swap(ids)
-    mine, own, rest = gate_dots(
-        core, ids, other_ids, other, got, other_rest, activations, out_grad
-    )
+    mine, own = gate_dots(core, ids, other_ids, other, got, activations, out_grad)
+    mine, own_rest, other_rest = lax.optimization_barrier((mine, own_rest, other_rest))
+    theirs = swap(mine)
+    rest = stage(own_rest, other_rest)
     score_grad, part = call(
         score_kernel,
         "scores",
@@ -341,14 +369,14 @@
         ),
         core,
         mine,
-        swap(mine),
+        theirs,
         ids,
         other_ids,
         own,
         other,
         rest,
     )
-    order = [side * chips + chip for side in (0, 1) for chip in chip_order]
+    order = [side * chips + chip for side in (1, 0) for chip in chip_order]
     part = exchange(part, ("side", "chip"), order)
     summed = call(
         sum_kernel,

time: 91.4 us -> 91.2 us (level)
  waiting for transfers between devices: 30 us -> 28 us
  Pallas kernels: 10.8 us -> 12.6 us
    ppermute x5, waiting for transfers between devices: 3.97 us -> 2.77 us  [swap(): return lax.ppermute(x, 'core', [(0, 1), (1, 0)])]
    pallas_call x0 -> x1, Pallas kernels: none -> 1.18 us  [stage(): pl.pallas_call(stage_kernel, in_specs=[pl.BlockSpec(memory_space=pltpu.HB...]
    pallas_call x1, Pallas kernels: 1.33 us -> 2.46 us  [halves_for_other(): pl.pallas_call(halves_kernel, in_specs=[pl.BlockSpec(memory_space=pltpu.S...]
  transfers between devices with their start and end apart: 7 -> 7, of which waited for: 5 -> 4; matrix products, arithmetic and copies ran while one was open for 0% -> 0% of each run, Pallas kernels for 3% -> 8%
where the time goes in v6:
time: 91.2 us; the launch traced here: 90.4 us
  starting transfers between devices  34.1 us (37%)
  waiting for transfers between devices  28 us (31%)
  blocking collectives  14.9 us (16%)
  Pallas kernels  12.6 us (14%)
    all_to_all x2, waiting for transfers between devices, exchange(): lax.all_to_all(x, axes, split_axis=0, concat_axis=0, tiled=True, axis_ind...  25.2 us
    all_to_all x2, starting transfers between devices, exchange(): lax.all_to_all(x, axes, split_axis=0, concat_axis=0, tiled=True, axis_ind...  23.9 us
    all_to_all x1, blocking collectives, exchange(): lax.all_to_all(x, axes, split_axis=0, concat_axis=0, tiled=True, axis_ind...  14.9 us
    ppermute x5, starting transfers between devices, swap(): return lax.ppermute(x, 'core', [(0, 1), (1, 0)])  10.2 us
    pallas_call x4, Pallas kernels, call(): pl.pallas_call(kernel, in_specs=[pl.BlockSpec(memory_space=pltpu.SMEM if...  4 us
    pallas_call x1, Pallas kernels, pack(): pl.pallas_call(pack_kernel, in_specs=[pl.BlockSpec(memory_space=pltpu.HBM...  3.1 us
    ppermute x5, waiting for transfers between devices, swap(): return lax.ppermute(x, 'core', [(0, 1), (1, 0)])  2.77 us
    pallas_call x1, Pallas kernels, halves_for_other(): pl.pallas_call(halves_kernel, in_specs=[pl.BlockSpec(memory_space=pltpu.S...  2.46 us
  transfers between devices with their start and end apart: 7, of which 4 were waited for; matrix products, arithmetic and copies ran while one was open for 0% of the time, Pallas kernels for 8%

profile of v6, /device:TPU:6, one launch (start us, length us, event | category | flops | bytes accessed | tf_op | source)
XLA Modules:
  0.0 90.4 jit_solution(5095900556083016663)
XLA Ops:
  0.6 3.1 %pack_rows.1 = bf16[256,4480]{1,0:T(8,128)(2,1)} custom-call(bf16[256,3584]{1,0:T(8,128)(2,1)} %bitcast.21, bf16[4,3584]{1,0:T(4,128)(2,1)} %weight_hbm.1), custom_call_target="tpu_custom_call" | custom-call | tf_op jit(solution)/shard_map/pack_rows/pallas_call | solution.py:77
  3.7 0.0 copy-start
  3.8 10.3 %all-to-all-start = ((bf16[32,8,4480]{2,1,0:T(8,128)(2,1)}), bf16[32,8,4480]{2,1,0:T(8,128)(2,1)S(1)}, u32[]{:S(2)}, u32[]{:S(2)}) async-start(bf16[32,8,4480]{2,1,0:T(8,128)(2,1)} %bitcast.20), calls=%async_computation | async-start | bytes 4587520 | tf_op jit(solution)/shard_map/all_to_all | solution.py:335
  14.1 2.5 %halves_for_other.1 = (bf16[256,1792]{1,0:T(8,128)(2,1)S(1)}, bf16[128,1792]{1,0:T(8,128)(2,1)}, bf16[128,1792]{1,0:T(8,128)(2,1)}) custom-call(s32[1]{0:T(128)} %bitcast.core_ref, bf16[128,3584]{1,0:T(8,128)(2,1)} %act_hbm.3, bf16[128,3584]{1,0:T(8,128)(2,1)} %grad_hbm.3), custom_call_target="tpu_custom_call" | custom-call | tf_op jit(solution)/shard_map/halves_for_other/pallas_call | solution.py:127
  16.6 2.0 %collective-permute-start.1 = (bf16[256,1792]{1,0:T(8,128)(2,1)S(1)}, bf16[256,1792]{1,0:T(8,128)(2,1)S(1)}, u32[]{:S(2)}, u32[]{:S(2)}) collective-permute-start(bf16[256,1792]{1,0:T(8,128)(2,1)S(1)} %get-tuple-element.15), channel_id=1, source_target_pairs={{0,1},{1,0},{2,3},{3,2},{4,5},{5,4},{6,7},{7,6},{8,9},{9,8},{10,11... | collective-permute-start | bytes 2752520 | tf_op jit(solution)/shard_map/ppermute | solution.py:351
  18.6 2.3 %collective-permute-start.2 = (bf16[128,1792]{1,0:T(8,128)(2,1)}, bf16[128,1792]{1,0:T(8,128)(2,1)}, u32[]{:S(2)}, u32[]{:S(2)}) collective-permute-start(bf16[128,1792]{1,0:T(8,128)(2,1)} %get-tuple-element.18), channel_id=1, source_target_pairs={{0,1},{1,0},{2,3},{3,2},{4,5},{5,4},{6,7},{7,6},{8,9},{9,8},{10,11... | collective-permute-start | bytes 1376264 | tf_op jit(solution)/shard_map/ppermute | solution.py:351
  20.9 0.0 copy-done
  20.9 2.0 %collective-permute-start = (s32[2,128]{1,0:T(2,128)S(1)}, s32[2,128]{1,0:T(2,128)S(1)}, u32[]{:S(2)}, u32[]{:S(2)}) collective-permute-start(s32[2,128]{1,0:T(2,128)S(1)} %bitcast.15), channel_id=1, source_target_pairs={{0,1},{1,0},{2,3},{3,2},{4,5},{5,4},{6,7},{7,6},{8,9},{9,8},{10,11... | collective-permute-start | bytes 3080 | tf_op jit(solution)/shard_map/ppermute | solution.py:351
  23.0 1.0 %collective-permute-done.other_ids_ref = s32[2,128]{1,0:T(2,128)S(1)} collective-permute-done((s32[2,128]{1,0:T(2,128)S(1)}, s32[2,128]{1,0:T(2,128)S(1)}, u32[]{:S(2)}, u32[]{:S(2)}) %collective-permute-start) | collective-permute-done | bytes 1056 | tf_op jit(solution)/shard_map/ppermute | solution.py:351
  23.9 0.0 collective-permute-done.1.other_ref
  23.9 18.4 %all-to-all-done = bf16[32,8,4480]{2,1,0:T(8,128)(2,1)S(1)} async-done(((bf16[32,8,4480]{2,1,0:T(8,128)(2,1)}), bf16[32,8,4480]{2,1,0:T(8,128)(2,1)S(1)}, u32[]{:S(2)}, u32[]{:S(2)}) %all-to-all-start) | async-done | bytes 2293792 | tf_op jit(solution)/shard_map/all_to_all | solution.py:335
  42.4 1.8 %gate_dots.1 = (f32[16,128]{1,0:T(8,128)S(1)}, bf16[256,1792]{1,0:T(8,128)(2,1)S(1)}) custom-call(s32[1]{0:T(128)} %bitcast.core_ref, s32[2,128]{1,0:T(2,128)S(1)} %bitcast.16, s32[2,128]{1,0:T(2,128)S(1)} %collective-permute-done.other_ids_ref, bf16[256,1792]{1,0:T(8,128)(2,1)S(1)} %collective-permute-done.1.other_ref, bf16[256,4480]{1,0:T(8,128)(2,1)S(1)} %bitcast.10, ...), custom_call_target="tpu_custom_call" | custom-call | tf_op jit(solution)/shard_map/gate_dots/pallas_call | solution.py:238
  44.2 0.0 collective-permute-done.2.other_hbm
  44.2 1.9 %collective-permute-start.3 = (f32[16,128]{1,0:T(8,128)S(1)}, f32[16,128]{1,0:T(8,128)S(1)}, u32[]{:S(2)}, u32[]{:S(2)}) collective-permute-start(f32[16,128]{1,0:T(8,128)S(1)} %get-tuple-element.19.mine_ref), channel_id=1, source_target_pairs={{0,1},{1,0},{2,3},{3,2},{4,5},{5,4},{6,7},{7,6},{8,9},{9,8},{10,11... | collective-permute-start | bytes 24584 | tf_op jit(solution)/shard_map/ppermute | solution.py:351
  46.2 1.2 %stage.1.rest_ref = bf16[256,1792]{1,0:T(8,128)(2,1)S(1)} custom-call(bf16[128,1792]{1,0:T(8,128)(2,1)} %get-tuple-element.21.own_hbm, bf16[128,1792]{1,0:T(8,128)(2,1)} %collective-permute-done.2.other_hbm), custom_call_target="tpu_custom_call" | custom-call | tf_op jit(solution)/shard_map/stage/pallas_call | solution.py:225
  47.4 0.0 collective-permute-done.3.theirs_ref
  47.4 0.7 scores.1
  48.1 0.0 copy-start.1
  48.1 14.9 %all_to_all.33 = bf16[32,8,896]{2,1,0:T(8,128)(2,1)S(1)} all-to-all(bf16[32,8,896]{2,1,0:T(8,128)(2,1)S(1)} %bitcast.14), channel_id=1, replica_groups={{52,54,56,58,60,62,32,34,36,38,40,42,44,46,48,50,20,22,24,26,28,30,0,2,..., dimensions={0} | all-to-all | bytes 917504 | tf_op jit(solution)/shard_map/all_to_all | solution.py:335
  63.0 0.9 %sum_chips.1 = bf16[128,896]{1,0:T(8,128)(2,1)} custom-call(bf16[256,896]{1,0:T(8,128)(2,1)S(1)} %bitcast.12), custom_call_target="tpu_custom_call" | custom-call | tf_op jit(solution)/shard_map/sum_chips/pallas_call | solution.py:322
  64.0 13.5 %all-to-all-start.2 = ((bf16[16,8,896]{2,1,0:T(8,128)(2,1)}), bf16[16,8,896]{2,1,0:T(8,128)(2,1)S(1)}, u32[]{:S(2)}, u32[]{:S(2)}) async-start(bf16[16,8,896]{2,1,0:T(8,128)(2,1)} %bitcast.8), calls=%async_computation.2 | async-start | bytes 458752 | tf_op jit(solution)/shard_map/all_to_all | solution.py:335
  77.6 1.9 %collective-permute-start.4 = (bf16[256,896]{1,0:T(8,128)(2,1)S(1)}, bf16[256,896]{1,0:T(8,128)(2,1)S(1)}, u32[]{:S(2)}, u32[]{:S(2)}) collective-permute-start(bf16[256,896]{1,0:T(8,128)(2,1)S(1)} %slice.3.own_ref), channel_id=1, source_target_pairs={{0,1},{1,0},{2,3},{3,2},{4,5},{5,4},{6,7},{7,6},{8,9},{9,8},{10,11... | collective-permute-start | bytes 1376264 | tf_op jit(solution)/shard_map/ppermute | solution.py:351
  79.5 1.8 %collective-permute-done.4.other_ref = bf16[256,896]{1,0:T(8,128)(2,1)S(1)} collective-permute-done((bf16[256,896]{1,0:T(8,128)(2,1)S(1)}, bf16[256,896]{1,0:T(8,128)(2,1)S(1)}, u32[]{:S(2)}, u32[]{:S(2)}) %collective-permute-start.4) | collective-permute-done | bytes 458784 | tf_op jit(solution)/shard_map/ppermute | solution.py:351
  81.3 0.0 copy-done.1
  81.3 1.5 %input_grads.1 = bf16[128,3584]{1,0:T(8,128)(2,1)} custom-call(s32[1]{0:T(128)} %bitcast.core_ref, s32[2,128]{1,0:T(2,128)S(1)} %bitcast.18, f32[2,128]{1,0:T(2,128)S(1)} %copy-done.1, bf16[256,896]{1,0:T(8,128)(2,1)S(1)} %slice.3.own_ref, bf16[256,896]{1,0:T(8,128)(2,1)S(1)} %collective-permute-done.4.other_ref), custom_call_target="tpu_custom_call" | custom-call | flops 234881024 | bytes 1835008 | tf_op jit(solution)/shard_map/input_grads/pallas_call | solution.py:322
  82.7 6.8 %all-to-all-done.2 = bf16[16,8,896]{2,1,0:T(8,128)(2,1)S(1)} async-done(((bf16[16,8,896]{2,1,0:T(8,128)(2,1)}), bf16[16,8,896]{2,1,0:T(8,128)(2,1)S(1)}, u32[]{:S(2)}, u32[]{:S(2)}) %all-to-all-start.2) | async-done | bytes 229408 | tf_op jit(solution)/shard_map/all_to_all | solution.py:335
  89.5 0.9 sum_batches.1
  (1 shorter events, 0.0 us)
Async XLA Ops:
  3.7 17.2 %copy-start = (s32[128,2]{0,1:T(2,128)S(1)}, s32[128,2]{0,1:T(2,128)}, u32[]{:S(2)}) copy-start(s32[128,2]{0,1:T(2,128)} %param.8) | copy-start | bytes 3076
  3.8 38.6 %all-to-all-start = ((bf16[32,8,4480]{2,1,0:T(8,128)(2,1)}), bf16[32,8,4480]{2,1,0:T(8,128)(2,1)S(1)}, u32[]{:S(2)}, u32[]{:S(2)}) async-start(bf16[32,8,4480]{2,1,0:T(8,128)(2,1)} %bitcast.20), calls=%async_computation | async-start | bytes 4587520 | tf_op jit(solution)/shard_map/all_to_all | solution.py:335
  16.6 7.4 %collective-permute-start.1 = (bf16[256,1792]{1,0:T(8,128)(2,1)S(1)}, bf16[256,1792]{1,0:T(8,128)(2,1)S(1)}, u32[]{:S(2)}, u32[]{:S(2)}) collective-permute-start(bf16[256,1792]{1,0:T(8,128)(2,1)S(1)} %get-tuple-element.15), channel_id=1, source_target_pairs={{0,1},{1,0},{2,3},{3,2},{4,5},{5,4},{6,7},{7,6},{8,9},{9,8},{10,11... | collective-permute-start | bytes 2752520 | tf_op jit(solution)/shard_map/ppermute | solution.py:351
  18.6 25.6 %collective-permute-start.2 = (bf16[128,1792]{1,0:T(8,128)(2,1)}, bf16[128,1792]{1,0:T(8,128)(2,1)}, u32[]{:S(2)}, u32[]{:S(2)}) collective-permute-start(bf16[128,1792]{1,0:T(8,128)(2,1)} %get-tuple-element.18), channel_id=1, source_target_pairs={{0,1},{1,0},{2,3},{3,2},{4,5},{5,4},{6,7},{7,6},{8,9},{9,8},{10,11... | collective-permute-start | bytes 1376264 | tf_op jit(solution)/shard_map/ppermute | solution.py:351
  20.9 3.0 %collective-permute-start = (s32[2,128]{1,0:T(2,128)S(1)}, s32[2,128]{1,0:T(2,128)S(1)}, u32[]{:S(2)}, u32[]{:S(2)}) collective-permute-start(s32[2,128]{1,0:T(2,128)S(1)} %bitcast.15), channel_id=1, source_target_pairs={{0,1},{1,0},{2,3},{3,2},{4,5},{5,4},{6,7},{7,6},{8,9},{9,8},{10,11... | collective-permute-start | bytes 3080 | tf_op jit(solution)/shard_map/ppermute | solution.py:351
  44.2 3.1 %collective-permute-start.3 = (f32[16,128]{1,0:T(8,128)S(1)}, f32[16,128]{1,0:T(8,128)S(1)}, u32[]{:S(2)}, u32[]{:S(2)}) collective-permute-start(f32[16,128]{1,0:T(8,128)S(1)} %get-tuple-element.19.mine_ref), channel_id=1, source_target_pairs={{0,1},{1,0},{2,3},{3,2},{4,5},{5,4},{6,7},{7,6},{8,9},{9,8},{10,11... | collective-permute-start | bytes 24584 | tf_op jit(solution)/shard_map/ppermute | solution.py:351
  48.1 33.2 %copy-start.1 = (f32[2,128]{1,0:T(2,128)S(1)}, f32[2,128]{1,0:T(2,128)}, u32[]{:S(2)}) copy-start(f32[2,128]{1,0:T(2,128)} %get-tuple-element.23.score_grad_ref) | copy-start | bytes 3076
  64.0 25.5 %all-to-all-start.2 = ((bf16[16,8,896]{2,1,0:T(8,128)(2,1)}), bf16[16,8,896]{2,1,0:T(8,128)(2,1)S(1)}, u32[]{:S(2)}, u32[]{:S(2)}) async-start(bf16[16,8,896]{2,1,0:T(8,128)(2,1)} %bitcast.8), calls=%async_computation.2 | async-start | bytes 458752 | tf_op jit(solution)/shard_map/all_to_all | solution.py:335
  77.6 3.7 %collective-permute-start.4 = (bf16[256,896]{1,0:T(8,128)(2,1)S(1)}, bf16[256,896]{1,0:T(8,128)(2,1)S(1)}, u32[]{:S(2)}, u32[]{:S(2)}) collective-permute-start(bf16[256,896]{1,0:T(8,128)(2,1)S(1)} %slice.3.own_ref), channel_id=1, source_target_pairs={{0,1},{1,0},{2,3},{3,2},{4,5},{5,4},{6,7},{7,6},{8,9},{9,8},{10,11... | collective-permute-start | bytes 1376264 | tf_op jit(solution)/shard_map/ppermute | solution.py:351

commit v7 on v6

--- a/solution.py
+++ b/solution.py
@@ -303,19 +303,22 @@
 
 def sum_kernel(got_ref, out_ref):
     rows, sources = out_ref.shape[0], got_ref.shape[0]
-    pick = ones_where((iota((rows, sources), 0) & 7) == (iota((rows, sources), 1) & 7))
-    out_ref[...] = jnp.dot(pick, got_ref[...], preferred_element_type=F32).astype(BF16)
+    pick = ones_where((iota((16, sources), 0) & 7) == (iota((16, sources), 1) & 7))
+    total = jnp.dot(pick, got_ref[...], preferred_element_type=F32).astype(BF16)
+    for start in range(0, rows, 16):
+        out_ref[start : start + 16, :] = total
 
 
 def final_kernel(got_ref, out_ref):
     experts = out_ref.shape[0]
     sources, block = got_ref.shape
-    row, col = iota((experts, sources), 0), iota((experts, sources), 1)
+    row, col = iota((4 * experts, sources), 0), iota((4 * experts, sources), 1)
+    want = (row >> 3) * 8 + (row & 3) * 2 + ((row >> 2) & 1)
+    total = jnp.dot(ones_where((col & 15) == want), got_ref[...], preferred_element_type=F32)
     for piece in range(4):
-        pick = ones_where((col & 15) == ((piece >> 1) * 8 + row * 2 + (piece & 1)))
-        out_ref[:, piece * block : (piece + 1) * block] = jnp.dot(
-            pick, got_ref[...], preferred_element_type=F32
-        )
+        out_ref[:, piece * block : (piece + 1) * block] = total[
+            piece * experts : (piece + 1) * experts
+        ]
 
 
 def call(kernel, name, out_shape, *args, cost=None):

time: 91.2 us -> 91 us (level)
  no operation moved by 1% of the time
where the time goes in v7:
time: 91 us; the launch traced here: 90.2 us
  starting transfers between devices  34.1 us (37%)
  waiting for transfers between devices  28 us (31%)
  blocking collectives  14.9 us (16%)
  Pallas kernels  12.4 us (14%)
    all_to_all x2, waiting for transfers between devices, exchange(): lax.all_to_all(x, axes, split_axis=0, concat_axis=0, tiled=True, axis_ind...  25.2 us
    all_to_all x2, starting transfers between devices, exchange(): lax.all_to_all(x, axes, split_axis=0, concat_axis=0, tiled=True, axis_ind...  23.9 us
    all_to_all x1, blocking collectives, exchange(): lax.all_to_all(x, axes, split_axis=0, concat_axis=0, tiled=True, axis_ind...  14.9 us
    ppermute x5, starting transfers between devices, swap(): return lax.ppermute(x, 'core', [(0, 1), (1, 0)])  10.2 us
    pallas_call x4, Pallas kernels, call(): pl.pallas_call(kernel, in_specs=[pl.BlockSpec(memory_space=pltpu.SMEM if...  3.85 us
    pallas_call x1, Pallas kernels, pack(): pl.pallas_call(pack_kernel, in_specs=[pl.BlockSpec(memory_space=pltpu.HBM...  3.1 us
    ppermute x5, waiting for transfers between devices, swap(): return lax.ppermute(x, 'core', [(0, 1), (1, 0)])  2.77 us
    pallas_call x1, Pallas kernels, halves_for_other(): pl.pallas_call(halves_kernel, in_specs=[pl.BlockSpec(memory_space=pltpu.S...  2.46 us
  transfers between devices with their start and end apart: 7, of which 4 were waited for; matrix products, arithmetic and copies ran while one was open for 0% of the time, Pallas kernels for 8%

profile of v7, /device:TPU:6, one launch (start us, length us, event | category | flops | bytes accessed | tf_op | source)
XLA Modules:
  0.0 90.2 jit_solution(2989791770678266333)
XLA Ops:
  0.6 3.1 %pack_rows.1 = bf16[256,4480]{1,0:T(8,128)(2,1)} custom-call(bf16[256,3584]{1,0:T(8,128)(2,1)} %bitcast.21, bf16[4,3584]{1,0:T(4,128)(2,1)} %weight_hbm.1), custom_call_target="tpu_custom_call" | custom-call | tf_op jit(solution)/shard_map/pack_rows/pallas_call | solution.py:77
  3.7 0.0 copy-start
  3.8 10.3 %all-to-all-start = ((bf16[32,8,4480]{2,1,0:T(8,128)(2,1)}), bf16[32,8,4480]{2,1,0:T(8,128)(2,1)S(1)}, u32[]{:S(2)}, u32[]{:S(2)}) async-start(bf16[32,8,4480]{2,1,0:T(8,128)(2,1)} %bitcast.20), calls=%async_computation | async-start | bytes 4587520 | tf_op jit(solution)/shard_map/all_to_all | solution.py:338
  14.1 2.5 %halves_for_other.1 = (bf16[256,1792]{1,0:T(8,128)(2,1)S(1)}, bf16[128,1792]{1,0:T(8,128)(2,1)}, bf16[128,1792]{1,0:T(8,128)(2,1)}) custom-call(s32[1]{0:T(128)} %bitcast.core_ref, bf16[128,3584]{1,0:T(8,128)(2,1)} %act_hbm.3, bf16[128,3584]{1,0:T(8,128)(2,1)} %grad_hbm.3), custom_call_target="tpu_custom_call" | custom-call | tf_op jit(solution)/shard_map/halves_for_other/pallas_call | solution.py:127
  16.6 2.0 %collective-permute-start.1 = (bf16[256,1792]{1,0:T(8,128)(2,1)S(1)}, bf16[256,1792]{1,0:T(8,128)(2,1)S(1)}, u32[]{:S(2)}, u32[]{:S(2)}) collective-permute-start(bf16[256,1792]{1,0:T(8,128)(2,1)S(1)} %get-tuple-element.15), channel_id=1, source_target_pairs={{0,1},{1,0},{2,3},{3,2},{4,5},{5,4},{6,7},{7,6},{8,9},{9,8},{10,11... | collective-permute-start | bytes 2752520 | tf_op jit(solution)/shard_map/ppermute | solution.py:354
  18.6 2.3 %collective-permute-start.2 = (bf16[128,1792]{1,0:T(8,128)(2,1)}, bf16[128,1792]{1,0:T(8,128)(2,1)}, u32[]{:S(2)}, u32[]{:S(2)}) collective-permute-start(bf16[128,1792]{1,0:T(8,128)(2,1)} %get-tuple-element.18), channel_id=1, source_target_pairs={{0,1},{1,0},{2,3},{3,2},{4,5},{5,4},{6,7},{7,6},{8,9},{9,8},{10,11... | collective-permute-start | bytes 1376264 | tf_op jit(solution)/shard_map/ppermute | solution.py:354
  20.9 0.0 copy-done
  20.9 2.0 %collective-permute-start = (s32[2,128]{1,0:T(2,128)S(1)}, s32[2,128]{1,0:T(2,128)S(1)}, u32[]{:S(2)}, u32[]{:S(2)}) collective-permute-start(s32[2,128]{1,0:T(2,128)S(1)} %bitcast.15), channel_id=1, source_target_pairs={{0,1},{1,0},{2,3},{3,2},{4,5},{5,4},{6,7},{7,6},{8,9},{9,8},{10,11... | collective-permute-start | bytes 3080 | tf_op jit(solution)/shard_map/ppermute | solution.py:354
  23.0 1.0 %collective-permute-done.other_ids_ref = s32[2,128]{1,0:T(2,128)S(1)} collective-permute-done((s32[2,128]{1,0:T(2,128)S(1)}, s32[2,128]{1,0:T(2,128)S(1)}, u32[]{:S(2)}, u32[]{:S(2)}) %collective-permute-start) | collective-permute-done | bytes 1056 | tf_op jit(solution)/shard_map/ppermute | solution.py:354
  23.9 0.0 collective-permute-done.1.other_ref
  23.9 18.4 %all-to-all-done = bf16[32,8,4480]{2,1,0:T(8,128)(2,1)S(1)} async-done(((bf16[32,8,4480]{2,1,0:T(8,128)(2,1)}), bf16[32,8,4480]{2,1,0:T(8,128)(2,1)S(1)}, u32[]{:S(2)}, u32[]{:S(2)}) %all-to-all-start) | async-done | bytes 2293792 | tf_op jit(solution)/shard_map/all_to_all | solution.py:338
  42.4 1.8 %gate_dots.1 = (f32[16,128]{1,0:T(8,128)S(1)}, bf16[256,1792]{1,0:T(8,128)(2,1)S(1)}) custom-call(s32[1]{0:T(128)} %bitcast.core_ref, s32[2,128]{1,0:T(2,128)S(1)} %bitcast.16, s32[2,128]{1,0:T(2,128)S(1)} %collective-permute-done.other_ids_ref, bf16[256,1792]{1,0:T(8,128)(2,1)S(1)} %collective-permute-done.1.other_ref, bf16[256,4480]{1,0:T(8,128)(2,1)S(1)} %bitcast.10, ...), custom_call_target="tpu_custom_call" | custom-call | tf_op jit(solution)/shard_map/gate_dots/pallas_call | solution.py:238
  44.2 0.0 collective-permute-done.2.other_hbm
  44.2 1.9 %collective-permute-start.3 = (f32[16,128]{1,0:T(8,128)S(1)}, f32[16,128]{1,0:T(8,128)S(1)}, u32[]{:S(2)}, u32[]{:S(2)}) collective-permute-start(f32[16,128]{1,0:T(8,128)S(1)} %get-tuple-element.19.mine_ref), channel_id=1, source_target_pairs={{0,1},{1,0},{2,3},{3,2},{4,5},{5,4},{6,7},{7,6},{8,9},{9,8},{10,11... | collective-permute-start | bytes 24584 | tf_op jit(solution)/shard_map/ppermute | solution.py:354
  46.2 1.2 %stage.1.rest_ref = bf16[256,1792]{1,0:T(8,128)(2,1)S(1)} custom-call(bf16[128,1792]{1,0:T(8,128)(2,1)} %get-tuple-element.21.own_hbm, bf16[128,1792]{1,0:T(8,128)(2,1)} %collective-permute-done.2.other_hbm), custom_call_target="tpu_custom_call" | custom-call | tf_op jit(solution)/shard_map/stage/pallas_call | solution.py:225
  47.4 0.0 collective-permute-done.3.theirs_ref
  47.4 0.7 scores.1
  48.1 0.0 copy-start.1
  48.1 14.9 %all_to_all.33 = bf16[32,8,896]{2,1,0:T(8,128)(2,1)S(1)} all-to-all(bf16[32,8,896]{2,1,0:T(8,128)(2,1)S(1)} %bitcast.14), channel_id=1, replica_groups={{52,54,56,58,60,62,32,34,36,38,40,42,44,46,48,50,20,22,24,26,28,30,0,2,..., dimensions={0} | all-to-all | bytes 917504 | tf_op jit(solution)/shard_map/all_to_all | solution.py:338
  63.0 0.9 sum_chips.1
  63.9 13.5 %all-to-all-start.2 = ((bf16[16,8,896]{2,1,0:T(8,128)(2,1)}), bf16[16,8,896]{2,1,0:T(8,128)(2,1)S(1)}, u32[]{:S(2)}, u32[]{:S(2)}) async-start(bf16[16,8,896]{2,1,0:T(8,128)(2,1)} %bitcast.8), calls=%async_computation.2 | async-start | bytes 458752 | tf_op jit(solution)/shard_map/all_to_all | solution.py:338
  77.5 1.9 %collective-permute-start.4 = (bf16[256,896]{1,0:T(8,128)(2,1)S(1)}, bf16[256,896]{1,0:T(8,128)(2,1)S(1)}, u32[]{:S(2)}, u32[]{:S(2)}) collective-permute-start(bf16[256,896]{1,0:T(8,128)(2,1)S(1)} %slice.3.own_ref), channel_id=1, source_target_pairs={{0,1},{1,0},{2,3},{3,2},{4,5},{5,4},{6,7},{7,6},{8,9},{9,8},{10,11... | collective-permute-start | bytes 1376264 | tf_op jit(solution)/shard_map/ppermute | solution.py:354
  79.4 1.8 %collective-permute-done.4.other_ref = bf16[256,896]{1,0:T(8,128)(2,1)S(1)} collective-permute-done((bf16[256,896]{1,0:T(8,128)(2,1)S(1)}, bf16[256,896]{1,0:T(8,128)(2,1)S(1)}, u32[]{:S(2)}, u32[]{:S(2)}) %collective-permute-start.4) | collective-permute-done | bytes 458784 | tf_op jit(solution)/shard_map/ppermute | solution.py:354
  81.2 0.0 copy-done.1
  81.2 1.5 %input_grads.1 = bf16[128,3584]{1,0:T(8,128)(2,1)} custom-call(s32[1]{0:T(128)} %bitcast.core_ref, s32[2,128]{1,0:T(2,128)S(1)} %bitcast.18, f32[2,128]{1,0:T(2,128)S(1)} %copy-done.1, bf16[256,896]{1,0:T(8,128)(2,1)S(1)} %slice.3.own_ref, bf16[256,896]{1,0:T(8,128)(2,1)S(1)} %collective-permute-done.4.other_ref), custom_call_target="tpu_custom_call" | custom-call | flops 234881024 | bytes 1835008 | tf_op jit(solution)/shard_map/input_grads/pallas_call | solution.py:325
  82.7 6.8 %all-to-all-done.2 = bf16[16,8,896]{2,1,0:T(8,128)(2,1)S(1)} async-done(((bf16[16,8,896]{2,1,0:T(8,128)(2,1)}), bf16[16,8,896]{2,1,0:T(8,128)(2,1)S(1)}, u32[]{:S(2)}, u32[]{:S(2)}) %all-to-all-start.2) | async-done | bytes 229408 | tf_op jit(solution)/shard_map/all_to_all | solution.py:338
  89.5 0.8 sum_batches.1
  (1 shorter events, 0.0 us)
Async XLA Ops:
  3.7 17.2 %copy-start = (s32[128,2]{0,1:T(2,128)S(1)}, s32[128,2]{0,1:T(2,128)}, u32[]{:S(2)}) copy-start(s32[128,2]{0,1:T(2,128)} %param.8) | copy-start | bytes 3076
  3.8 38.6 %all-to-all-start = ((bf16[32,8,4480]{2,1,0:T(8,128)(2,1)}), bf16[32,8,4480]{2,1,0:T(8,128)(2,1)S(1)}, u32[]{:S(2)}, u32[]{:S(2)}) async-start(bf16[32,8,4480]{2,1,0:T(8,128)(2,1)} %bitcast.20), calls=%async_computation | async-start | bytes 4587520 | tf_op jit(solution)/shard_map/all_to_all | solution.py:338
  16.6 7.4 %collective-permute-start.1 = (bf16[256,1792]{1,0:T(8,128)(2,1)S(1)}, bf16[256,1792]{1,0:T(8,128)(2,1)S(1)}, u32[]{:S(2)}, u32[]{:S(2)}) collective-permute-start(bf16[256,1792]{1,0:T(8,128)(2,1)S(1)} %get-tuple-element.15), channel_id=1, source_target_pairs={{0,1},{1,0},{2,3},{3,2},{4,5},{5,4},{6,7},{7,6},{8,9},{9,8},{10,11... | collective-permute-start | bytes 2752520 | tf_op jit(solution)/shard_map/ppermute | solution.py:354
  18.6 25.6 %collective-permute-start.2 = (bf16[128,1792]{1,0:T(8,128)(2,1)}, bf16[128,1792]{1,0:T(8,128)(2,1)}, u32[]{:S(2)}, u32[]{:S(2)}) collective-permute-start(bf16[128,1792]{1,0:T(8,128)(2,1)} %get-tuple-element.18), channel_id=1, source_target_pairs={{0,1},{1,0},{2,3},{3,2},{4,5},{5,4},{6,7},{7,6},{8,9},{9,8},{10,11... | collective-permute-start | bytes 1376264 | tf_op jit(solution)/shard_map/ppermute | solution.py:354
  20.9 3.0 %collective-permute-start = (s32[2,128]{1,0:T(2,128)S(1)}, s32[2,128]{1,0:T(2,128)S(1)}, u32[]{:S(2)}, u32[]{:S(2)}) collective-permute-start(s32[2,128]{1,0:T(2,128)S(1)} %bitcast.15), channel_id=1, source_target_pairs={{0,1},{1,0},{2,3},{3,2},{4,5},{5,4},{6,7},{7,6},{8,9},{9,8},{10,11... | collective-permute-start | bytes 3080 | tf_op jit(solution)/shard_map/ppermute | solution.py:354
  44.2 3.1 %collective-permute-start.3 = (f32[16,128]{1,0:T(8,128)S(1)}, f32[16,128]{1,0:T(8,128)S(1)}, u32[]{:S(2)}, u32[]{:S(2)}) collective-permute-start(f32[16,128]{1,0:T(8,128)S(1)} %get-tuple-element.19.mine_ref), channel_id=1, source_target_pairs={{0,1},{1,0},{2,3},{3,2},{4,5},{5,4},{6,7},{7,6},{8,9},{9,8},{10,11... | collective-permute-start | bytes 24584 | tf_op jit(solution)/shard_map/ppermute | solution.py:354
  48.1 33.1 %copy-start.1 = (f32[2,128]{1,0:T(2,128)S(1)}, f32[2,128]{1,0:T(2,128)}, u32[]{:S(2)}) copy-start(f32[2,128]{1,0:T(2,128)} %get-tuple-element.23.score_grad_ref) | copy-start | bytes 3076
  63.9 25.5 %all-to-all-start.2 = ((bf16[16,8,896]{2,1,0:T(8,128)(2,1)}), bf16[16,8,896]{2,1,0:T(8,128)(2,1)S(1)}, u32[]{:S(2)}, u32[]{:S(2)}) async-start(bf16[16,8,896]{2,1,0:T(8,128)(2,1)} %bitcast.8), calls=%async_computation.2 | async-start | bytes 458752 | tf_op jit(solution)/shard_map/all_to_all | solution.py:338
  77.5 3.7 %collective-permute-start.4 = (bf16[256,896]{1,0:T(8,128)(2,1)S(1)}, bf16[256,896]{1,0:T(8,128)(2,1)S(1)}, u32[]{:S(2)}, u32[]{:S(2)}) collective-permute-start(bf16[256,896]{1,0:T(8,128)(2,1)S(1)} %slice.3.own_ref), channel_id=1, source_target_pairs={{0,1},{1,0},{2,3},{3,2},{4,5},{5,4},{6,7},{7,6},{8,9},{9,8},{10,11... | collective-permute-start | bytes 1376264 | tf_op jit(solution)/shard_map/ppermute | solution.py:354
